TPU v7x, 128 devices: a whole 4x4x4 slice. The times are simulated.
128 devices in a mesh: sec: 4 (over z_hi, core), dp: 32 (over y, x, z_lo).
Axes of the slice: x: 4, y: 4, z: 4 (z_hi: 2, z_lo: 2; z = z_hi * 2 + z_lo), core: 2. Of those that a mesh axis runs over, the one named last changes fastest.
Arguments:
- candidate_hidden_states: bfloat16 [64, 128, 2048], P('dp'), may hold values from -6 to 6
- kept_candidate_index: int32 [64, 128], P('dp'), may hold values from 0 to 127, each once within a row
- slot_parent_beam: int32 [64, 128], P('dp'), may hold values from 0 to 127
- alive_slot_counts: int32 [64], P('dp'), may hold values from 64 to 128, as said below
- slot_expert_index: int32 [64, 128, 2], P('dp'), may hold values from 0 to 31, all different within a row; in each aligned block of 256 rows (0 to 255, 256 to 511, ..., all dimensions but the last counted through in order) at most 24 rows name the same one
- attention_norm_gain: float32 [2048], replicated, may hold values from 0.1 to 1.9
- query_projection_weight: bfloat16 [2048, 2048], P(None, 'sec'), may hold values from -0.125 to 0.125
- key_projection_weight: bfloat16 [2048, 2048], P(None, 'sec'), may hold values from -0.4375 to 0.4375
- value_projection_weight: bfloat16 [2048, 2048], P(None, 'sec'), may hold values from -0.125 to 0.125
- attention_output_weight: bfloat16 [2048, 2048], P('sec'), may hold values from -0.125 to 0.125
- history_event_keys: bfloat16 [64, 2048, 2048], P('dp', None, 'sec'), may hold values from -48 to 48
- history_event_values: bfloat16 [64, 2048, 2048], P('dp', None, 'sec'), may hold values from -6 to 6
- decoded_beam_keys: bfloat16 [64, 128, 2, 2048], P('dp', None, None, 'sec'), may hold values from -16 to 16
- decoded_beam_values: bfloat16 [64, 128, 2, 2048], P('dp', None, None, 'sec'), may hold values from -6 to 6
- expert_norm_gain: float32 [2048], replicated, may hold values from 0.1 to 1.9
- router_projection_weight: bfloat16 [2048, 32], replicated, may hold values from -0.125 to 0.125
- expert_gate_weight: bfloat16 [32, 2048, 2048], P('dp', None, 'sec'), may hold values from -0.125 to 0.125
- expert_up_weight: bfloat16 [32, 2048, 2048], P('dp', None, 'sec'), may hold values from -0.125 to 0.125
- expert_down_weight: bfloat16 [32, 2048, 2048], P('dp', 'sec'), may hold values from -0.125 to 0.125
Outputs:
- output: bfloat16 [64, 128, 2048], P('dp', None, 'sec')
Inputs may be any that keep to these rules, and one draw needn't show every extreme that they name: The first alive_slot_counts[u] slots of user u are live; at least one user has all 128 slots live and one has 64. `kept_candidate_index`: each user's row lists every candidate once. `slot_expert_index`: the 2 experts of a slot differ; among the 256 slots of one index of dp (dead slots included) no expert is named more than 24 times, and in every draw some index of dp has an expert named exactly 24 times.
All inputs are finite; a program needn't handle non-finite values.
Results may differ from a plain program's by a relative error of at most 0.012.
Values may be sent and summed in bfloat16 or wider, within the bound.
No kernel may reach another device: no remote copies, remote signals or barrier semaphores. Data moves between devices by JAX's collectives and lax.ppermute only.
A program may use at most 128 MiB of HBM per device.

v0:
```python
import jax
import jax.numpy as jnp
from jax import lax
from jax.sharding import PartitionSpec as P

HD = 128


EPSILON = 1e-05


def rms_scale(values, gain):
    mean_square = jnp.mean(values * values, axis=-1, keepdims=True)
    return values * lax.rsqrt(mean_square + EPSILON) * gain


def on_device(
    candidate_hidden_states,
    kept_candidate_index,
    slot_parent_beam,
    alive_slot_counts,
    slot_expert_index,
    attention_norm_gain,
    query_projection_weight,
    key_projection_weight,
    value_projection_weight,
    attention_output_weight,
    history_event_keys,
    history_event_values,
    decoded_beam_keys,
    decoded_beam_values,
    expert_norm_gain,
    router_projection_weight,
    expert_gate_weight,
    expert_up_weight,
    expert_down_weight,
):
    user_count = candidate_hidden_states.shape[0]
    beam_slot_count = candidate_hidden_states.shape[1]
    width_full = candidate_hidden_states.shape[2]
    total_row_count = user_count * beam_slot_count
    local_feat = query_projection_weight.shape[1]
    head_count = local_feat // HD
    history = history_event_keys.shape[1]
    step_count = decoded_beam_keys.shape[2]
    sec_count = lax.axis_size("sec")
    dp_count = lax.axis_size("dp")
    experts = router_projection_weight.shape[1]
    top_count = slot_expert_index.shape[2]
    capacity = 3 * total_row_count * top_count // (2 * dp_count)
    quarter = width_full // sec_count
    sec_index = lax.axis_index("sec")
    score_scale = HD ** (-0.5)
    decoder_state = jnp.take_along_axis(
        candidate_hidden_states, kept_candidate_index[:, :, None], axis=1
    ).astype(jnp.float32)
    slot_is_alive = (
        jnp.arange(beam_slot_count, dtype=jnp.int32)[None, :] < alive_slot_counts[:, None]
    ).reshape(total_row_count)
    past_keys = jnp.take_along_axis(
        decoded_beam_keys, slot_parent_beam[:, :, None, None], axis=1
    ).reshape(user_count, beam_slot_count, step_count, head_count, HD)
    past_values = jnp.take_along_axis(
        decoded_beam_values, slot_parent_beam[:, :, None, None], axis=1
    ).reshape(user_count, beam_slot_count, step_count, head_count, HD)
    normed = (
        rms_scale(decoder_state, attention_norm_gain)
        .astype(jnp.bfloat16)
        .reshape(total_row_count, width_full)
    )
    query_rows = (
        jnp.dot(normed, query_projection_weight, preferred_element_type=jnp.float32)
        .astype(jnp.bfloat16)
        .reshape(user_count, beam_slot_count, head_count, HD)
    )
    new_key = (
        jnp.dot(normed, key_projection_weight, preferred_element_type=jnp.float32)
        .astype(jnp.bfloat16)
        .reshape(user_count, beam_slot_count, head_count, HD)
    )
    new_value = (
        jnp.dot(normed, value_projection_weight, preferred_element_type=jnp.float32)
        .astype(jnp.bfloat16)
        .reshape(user_count, beam_slot_count, head_count, HD)
    )
    keys_hist = history_event_keys.reshape(user_count, history, head_count, HD)
    values_hist = history_event_values.reshape(user_count, history, head_count, HD)
    score_hist = (
        jnp.einsum("ubhd,ukhd->ubhk", query_rows, keys_hist, preferred_element_type=jnp.float32)
        * score_scale
    )
    score_past = (
        jnp.einsum("ubhd,ubshd->ubhs", query_rows, past_keys, preferred_element_type=jnp.float32)
        * score_scale
    )
    score_new = (
        jnp.einsum("ubhd,ubhd->ubh", query_rows, new_key, preferred_element_type=jnp.float32)
        * score_scale
    )
    highest = jnp.maximum(
        jnp.maximum(jnp.max(score_hist, axis=-1), jnp.max(score_past, axis=-1)), score_new
    )
    exp_hist = jnp.exp(score_hist - highest[..., None])
    exp_past = jnp.exp(score_past - highest[..., None])
    exp_new = jnp.exp(score_new - highest)
    total_mass = jnp.sum(exp_hist, axis=-1) + jnp.sum(exp_past, axis=-1) + exp_new
    weight_hist = (exp_hist / total_mass[..., None]).astype(jnp.bfloat16)
    weight_past = (exp_past / total_mass[..., None]).astype(jnp.bfloat16)
    weight_new = (exp_new / total_mass).astype(jnp.bfloat16)
    attended = jnp.einsum(
        "ubhk,ukhd->ubhd", weight_hist, values_hist, preferred_element_type=jnp.float32
    )
    attended = attended + jnp.einsum(
        "ubhs,ubshd->ubhd", weight_past, past_values, preferred_element_type=jnp.float32
    )
    attended = attended + weight_new.astype(jnp.float32)[..., None] * new_value.astype(jnp.float32)
    attended = attended.astype(jnp.bfloat16).reshape(total_row_count, local_feat)
    partial_out = jnp.dot(attended, attention_output_weight, preferred_element_type=jnp.float32)
    flat_state = decoder_state.reshape(total_row_count, width_full)
    summed_heads = lax.psum(partial_out, "sec")
    resid_full = flat_state + summed_heads
    outgoing = rms_scale(resid_full, expert_norm_gain).astype(jnp.bfloat16)
    logits = jnp.dot(outgoing, router_projection_weight, preferred_element_type=jnp.float32)
    resid_part = lax.dynamic_slice_in_dim(resid_full, sec_index * quarter, quarter, 1)
    choice_ids = slot_expert_index.reshape(total_row_count, top_count)
    picked = jnp.take_along_axis(logits, choice_ids, axis=1)
    sigmoids = jax.nn.sigmoid(picked)
    gate_values = jnp.where(
        slot_is_alive[:, None], sigmoids / jnp.sum(sigmoids, axis=-1, keepdims=True), 0.0
    )
    onehot = (
        (choice_ids[:, :, None] == jnp.arange(experts, dtype=jnp.int32)[None, None, :])
        & slot_is_alive[:, None, None]
    ).astype(jnp.int32)
    onehot = onehot.reshape(total_row_count * top_count, experts)
    position = jnp.sum((jnp.cumsum(onehot, axis=0) - 1) * onehot, axis=1).reshape(
        total_row_count, top_count
    )
    slot_ids = choice_ids * capacity + position
    slot_range = jnp.arange(experts * capacity, dtype=jnp.int32)
    placing = jnp.any(
        (slot_ids[None, :, :] == slot_range[:, None, None]) & slot_is_alive[None, :, None], axis=2
    ).astype(jnp.bfloat16)
    bucket = jnp.dot(placing, outgoing, preferred_element_type=jnp.float32).astype(jnp.bfloat16)
    arrived = lax.all_to_all(bucket, "dp", split_axis=0, concat_axis=0, tiled=True)
    activated = jax.nn.silu(
        jnp.dot(arrived, expert_gate_weight[0], preferred_element_type=jnp.float32)
    ) * jnp.dot(arrived, expert_up_weight[0], preferred_element_type=jnp.float32)
    activated = activated.astype(jnp.bfloat16)
    partial_expert = jnp.dot(activated, expert_down_weight[0], preferred_element_type=jnp.float32)
    returned = lax.all_to_all(
        partial_expert.astype(jnp.bfloat16), "dp", split_axis=0, concat_axis=0, tiled=True
    ).astype(partial_expert.dtype)
    mixed_rows = jnp.sum(gate_values[:, :, None] * returned[slot_ids], axis=1)
    mixed_part = lax.psum_scatter(
        mixed_rows.astype(jnp.bfloat16), "sec", scatter_dimension=1, tiled=True
    ).astype(jnp.float32)
    output = jnp.where(slot_is_alive[:, None], resid_part + mixed_part, 0.0).astype(jnp.bfloat16)
    return output.reshape(user_count, beam_slot_count, quarter)


def solution(mesh):
    in_specs = (
        P("dp", None, None),
        P("dp", None),
        P("dp", None),
        P("dp"),
        P("dp", None, None),
        P(),
        P(None, "sec"),
        P(None, "sec"),
        P(None, "sec"),
        P("sec", None),
        P("dp", None, "sec"),
        P("dp", None, "sec"),
        P("dp", None, None, "sec"),
        P("dp", None, None, "sec"),
        P(),
        P(),
        P("dp", None, "sec"),
        P("dp", None, "sec"),
        P("dp", "sec", None),
    )
    out_specs = P("dp", None, "sec")
    return jax.shard_map(
        on_device, mesh=mesh, in_specs=in_specs, out_specs=out_specs, check_vma=False
    )
```

profile of v0, /device:TPU:1, one launch (start us, length us, event | category | flops | bytes accessed | tf_op | source)
XLA Modules:
  0.0 309.0 jit_solution(2126448872884783655)
XLA Ops:
  8.8 4.2 %gather_fusion.1 = bf16[256,2048]{1,0:T(8,128)(2,1)S(1)} fusion(bf16[2,128,2048]{2,1,0:T(8,128)(2,1)} %param.21, s32[256]{0:T(256)S(1)} %fusion.65), kind=kCustom, calls=%fused_computation.3 | custom fusion | bytes 2099200 | tf_op jit(solution)/shard_map/jit(take_along_axis)/gather | solution.py:54
  13.4 3.1 %convolution_convert_fusion.4 = bf16[256,512]{1,0:T(8,128)(2,1)} fusion(bf16[2048,512]{1,0:T(8,128)(2,1)} %param.27, f32[2048]{0:T(1024)S(1)} %copy-done.17, f32[256]{0:T(256)S(1)} %rsqrt_bitcast_fusion, bf16[256,2048]{1,0:T(8,128)(2,1)S(1)} %gather_fusion.1, pred[256]{0:T(512)(128)(4,1)S(1)} %fusion.84), kind=kOutput, calls=%fused_computation.42 | convolution fusion | flops 539623424 | bytes 3417344 | tf_op jit(solution)/shard_map/dot_general | solution.py:72
  17.5 3.1 %reshape.389 = bf16[2,128,4,128,1]{3,4,2,1,0:T(2,128)(2,1)} reshape(bf16[256,512]{1,0:T(8,128)(2,1)} %convolution_convert_fusion.4) | data formatting | bytes 524288 | tf_op jit(solution)/shard_map/reshape | solution.py:74
  20.7 3.9 %gather_fusion.3 = bf16[256,2,512]{2,1,0:T(2,128)(2,1)} fusion(bf16[2,128,2,512]{3,2,1,0:T(2,128)(2,1)} %param.33, s32[256]{0:T(256)S(1)} %fusion.64), kind=kCustom, calls=%fused_computation.clone | custom fusion | bytes 1050624 | tf_op jit(solution)/shard_map/jit(take_along_axis)/gather | solution.py:60
  24.5 3.4 %fusion.39 = f32[2,128,4,1,2]{4,3,2,1,0:T(1,128)} fusion(bf16[2,128,4,128,1]{3,4,2,1,0:T(2,128)(2,1)} %reshape.389, bf16[2,128,2,512]{3,2,1,0:T(2,128)(2,1)} %bitcast.180, pred[2,128]{1,0:T(4,128)(4,1)S(1)} %and_bitcast_fusion), kind=kOutput, calls=%fused_computation.54 | convolution fusion | flops 786432 | bytes 794880 | tf_op jit(solution)/shard_map/ubhd,ubshd->ubhs/dot_general | solution.py:93
  29.7 3.1 convolution_convert_fusion.3
  32.8 1.7 reshape.309
  34.5 6.7 %bitcast_reduce_fusion = (f32[2,128,4]{1,2,0:T(4,128)S(1)}, f32[2,4,128,2048]{3,2,1,0:T(8,128)}) fusion(bf16[2,128,4,128]{3,2,1,0:T(4,128)(2,1)S(1)} %reshape.306, bf16[2,2048,512]{2,1,0:T(8,128)(2,1)} %param.31), kind=kOutput, calls=%fused_computation.6 | convolution fusion | flops 541064192 | bytes 12849152 | tf_op jit(solution)/shard_map/ubhd,ukhd->ubhk/dot_general | solution.py:89
  42.4 4.3 %fusion.1 = f32[2,128,4]{1,2,0:T(4,128)S(1)} fusion(f32[2,4,128,2048]{3,2,1,0:T(8,128)} %get-tuple-element.13, f32[2,128,4]{1,2,0:T(4,128)S(1)} %maximum_maximum_fusion), kind=kLoop, calls=%fused_computation.9 | loop fusion | flops 6290432 | bytes 8396800 | tf_op jit(solution)/shard_map/reduce_sum | solution.py:106
  47.9 3.9 %gather_fusion.4 = bf16[256,2,512]{2,1,0:T(2,128)(2,1)} fusion(bf16[2,128,2,512]{3,2,1,0:T(2,128)(2,1)} %param.34, s32[256]{0:T(256)S(1)} %fusion.64), kind=kCustom, calls=%fused_computation.1.clone | custom fusion | bytes 1050624 | tf_op jit(solution)/shard_map/jit(take_along_axis)/gather | solution.py:63
  51.8 3.2 %fusion.31 = f32[256,512]{1,0:T(8,128)} fusion(bf16[2048,512]{1,0:T(8,128)(2,1)} %param.29, f32[2048]{0:T(1024)S(1)} %copy-done.18, f32[256]{0:T(256)S(1)} %copy-done.12, bf16[256,2048]{1,0:T(8,128)(2,1)S(1)} %gather_fusion.1, pred[256]{0:T(512)(128)(4,1)S(1)} %copy-done.14), kind=kOutput, calls=%fused_computation.43 | convolution fusion | flops 539754496 | bytes 3679488 | tf_op jit(solution)/shard_map/dot_general | solution.py:82
  55.0 2.0 reshape.320
  57.0 2.7 fusion.37
  59.7 5.0 %fusion.28 = bf16[2,128,4,128]{3,1,2,0:T(8,128)(2,1)S(1)} fusion(f32[2,4,128,2048]{3,2,1,0:T(8,128)} %get-tuple-element.13, f32[2,128,4]{1,2,0:T(4,128)S(1)} %get-tuple-element.9, f32[2,128,4]{1,2,0:T(4,128)S(1)} %maximum_maximum_fusion, f32[2,128,4,1,128]{4,3,2,1,0:T(1,128)S(1)} %fusion.37, f32[2,128,4,128]{3,2,1,0:T(4,128)S(1)} %copy-done.6, ...), kind=kOutput, calls=%fused_computation.39 | convolution fusion | flops 545783808 | bytes 13905920 | tf_op jit(solution)/shard_map/ubhk,ukhd->ubhd/dot_general | solution.py:110
  65.0 2.0 fusion.41
  69.1 1.2 reduce-window.6
  71.2 58.4 %all-reduce.2.cloned.1.call-done = f32[256,2048]{1,0:T(8,128)} async-done(((f32[256,2048]{1,0:T(8,128)}), f32[256,2048]{1,0:T(8,128)}) %all-reduce.2.cloned.1.call-update) | async-done | bytes 2097168 | tf_op jit(solution)/shard_map/psum | solution.py:120
  129.7 2.1 multiply_reduce_fusion.1
  133.1 46.3 %all_to_all.21 = bf16[32,24,2048]{2,1,0:T(8,128)(2,1)S(1)} all-to-all(bf16[32,24,2048]{2,1,0:T(8,128)(2,1)S(1)} %bitcast.173), channel_id=1, replica_groups=mesh['sec'=4,'dp'=32] {'dp'}, dimensions={0} | all-to-all | bytes 6291456 | tf_op jit(solution)/shard_map/all_to_all | solution.py:145
  179.4 1.7 copy-done.3
  181.1 2.9 fusion.13
  184.0 8.1 %convolution_convert_fusion = bf16[768,2048]{1,0:T(8,128)(2,1)} fusion(bf16[1,512,2048]{2,1,0:T(8,128)(2,1)S(1)} %copy-done, f32[768,512]{1,0:T(8,128)} %fusion.13, bf16[768,2048]{1,0:T(8,128)(2,1)} %bitcast.177, bf16[1,2048,512]{2,1,0:T(8,128)(2,1)} %param.38), kind=kOutput, calls=%fused_computation.17 | convolution fusion | flops 3225157632 | bytes 12058624 | tf_op jit(solution)/shard_map/dot_general | solution.py:150
  192.2 4.9 %all-to-all-start.1 = ((bf16[32,24,2048]{2,1,0:T(8,128)(2,1)}), bf16[32,24,2048]{2,1,0:T(8,128)(2,1)}, u32[]{:S(2)}, u32[]{:S(2)}) async-start(bf16[32,24,2048]{2,1,0:T(8,128)(2,1)} %bitcast.175), calls=%async_computation.1 | async-start | bytes 6291456 | tf_op jit(solution)/shard_map/all_to_all | solution.py:151
  198.0 2.1 fusion.70
  200.1 4.8 %gather_fusion.2 = f32[512]{0:T(512)S(1)} fusion(f32[256,32]{0,1:T(8,128)S(1)} %fusion.70, s32[512]{0:T(512)S(1)} %reshape.348), kind=kCustom, calls=%fused_computation.4 | custom fusion | bytes 8192 | tf_op jit(solution)/shard_map/jit(take_along_axis)/gather | solution.py:126
  205.5 32.5 %all-to-all-done.1 = bf16[32,24,2048]{2,1,0:T(8,128)(2,1)} async-done(((bf16[32,24,2048]{2,1,0:T(8,128)(2,1)}), bf16[32,24,2048]{2,1,0:T(8,128)(2,1)}, u32[]{:S(2)}, u32[]{:S(2)}) %all-to-all-start.1) | async-done | bytes 3145760 | tf_op jit(solution)/shard_map/all_to_all | solution.py:151
  238.0 5.4 %bitcast_convert_fusion = f32[768,2048]{1,0:T(8,128)} fusion(bf16[32,24,2048]{2,1,0:T(8,128)(2,1)} %all-to-all-done.1), kind=kLoop, calls=%fused_computation.19 | loop fusion | flops 1572864 | bytes 9437184 | tf_op jit(solution)/shard_map/convert_element_type | solution.py:153
  243.4 8.3 %gather_fusion = f32[512,2048]{1,0:T(8,128)} fusion(f32[768,2048]{1,0:T(8,128)} %bitcast_convert_fusion, s32[1024]{0:T(1024)S(1)} %pad_clamp_fusion), kind=kCustom, calls=%fused_computation.2 | custom fusion | bytes 8390656 | tf_op jit(solution)/shard_map/gather | solution.py:154
  251.7 5.8 %reshape.335 = f32[256,2,2048]{2,1,0:T(2,128)} reshape(f32[512,2048]{1,0:T(8,128)} %gather_fusion) | data formatting | bytes 8388608 | tf_op jit(solution)/shard_map/gather | solution.py:154
  257.5 10.0 %multiply_reduce_fusion = bf16[256,2048]{1,0:T(8,128)(2,1)} fusion(f32[256,2,2048]{2,1,0:T(2,128)} %reshape.335, f32[256,2]{1,0:T(8,128)S(1)} %copy.76), kind=kLoop, calls=%fused_computation.16 | loop fusion | flops 1572864 | bytes 5244928 | tf_op jit(solution)/shard_map/reduce_sum | solution.py:154
  267.5 32.5 %reduce-scatter.2.cloned.1.call-done = bf16[256,512]{1,0:T(8,128)(2,1)} async-done(((bf16[256,2048]{1,0:T(8,128)(2,1)}), bf16[256,512]{1,0:T(8,128)(2,1)}) %reduce-scatter.2.cloned.1.call-update) | async-done | bytes 262160 | tf_op jit(solution)/shard_map/reduce_scatter | solution.py:155
  300.0 1.9 select_convert_fusion
  (104 shorter events, 13.8 us)
Async XLA Ops:
  6.5 177.5 %copy-start = (bf16[1,512,2048]{2,1,0:T(8,128)(2,1)S(1)}, bf16[1,512,2048]{2,1,0:T(8,128)(2,1)}, u32[]{:S(2)}) copy-start(bf16[1,512,2048]{2,1,0:T(8,128)(2,1)} %param.39) | copy-start | bytes 6291460
  6.5 123.1 %all-reduce.2.cloned.1.call-start = ((), (), s32[]{:S(2)}) async-start(), calls=%async_computation.3 | async-start | bytes 4194304 | tf_op jit(solution)/shard_map/psum | solution.py:120
  8.7 20.9 %copy-start.13 = (pred[256]{0:T(512)(128)(4,1)}, pred[256]{0:T(512)(128)(4,1)S(1)}, u32[]{:S(2)}) copy-start(pred[256]{0:T(512)(128)(4,1)S(1)} %fusion.84) | copy-start | bytes 772
  8.7 4.6 %copy-start.17 = (f32[2048]{0:T(1024)S(1)}, f32[2048]{0:T(1024)}, u32[]{:S(2)}) copy-start(f32[2048]{0:T(1024)} %param.26) | copy-start | bytes 24580
  13.4 16.3 %copy-start.11 = (f32[256]{0:T(256)}, f32[256]{0:T(256)S(1)}, u32[]{:S(2)}) copy-start(f32[256]{0:T(256)S(1)} %rsqrt_bitcast_fusion) | copy-start | bytes 3076
  13.4 7.2 %copy-start.10 = (s32[2,128]{1,0:T(2,128)S(1)}, s32[2,128]{1,0:T(2,128)}, u32[]{:S(2)}) copy-start(s32[2,128]{1,0:T(2,128)} %param.23) | copy-start | bytes 3076
  20.6 7.2 %copy-start.20 = (pred[2,128]{1,0:T(4,128)(4,1)}, pred[2,128]{1,0:T(4,128)(4,1)S(1)}, u32[]{:S(2)}) copy-start(pred[2,128]{1,0:T(4,128)(4,1)S(1)} %and_bitcast_fusion) | copy-start | bytes 772
  34.5 6.7 %copy-start.5 = (bf16[2,128,4,128]{3,2,1,0:T(4,128)(2,1)S(1)}, bf16[2,128,4,128]{3,2,1,0:T(4,128)(2,1)}, u32[]{:S(2)}) copy-start(bf16[2,128,4,128]{3,2,1,0:T(4,128)(2,1)} %reshape.309) | copy-start | bytes 786436
  42.4 9.4 %copy-start.12 = (f32[256]{0:T(256)S(1)}, f32[256]{0:T(256)}, u32[]{:S(2)}) copy-start(f32[256]{0:T(256)} %copy-done.11) | copy-start | bytes 3076
  42.4 9.4 %copy-start.14 = (pred[256]{0:T(512)(128)(4,1)S(1)}, pred[256]{0:T(512)(128)(4,1)}, u32[]{:S(2)}) copy-start(pred[256]{0:T(512)(128)(4,1)} %copy-done.13) | copy-start | bytes 772
  42.4 9.4 %copy-start.18 = (f32[2048]{0:T(1024)S(1)}, f32[2048]{0:T(1024)}, u32[]{:S(2)}) copy-start(f32[2048]{0:T(1024)} %param.26) | copy-start | bytes 24580
  51.8 5.2 %copy-start.21 = (pred[2,128]{1,0:T(4,128)(4,1)S(1)}, pred[2,128]{1,0:T(4,128)(4,1)}, u32[]{:S(2)}) copy-start(pred[2,128]{1,0:T(4,128)(4,1)} %copy-done.20) | copy-start | bytes 772
  57.0 2.7 copy-start.6
  57.0 2.7 copy-start.15
  59.7 5.3 %copy-start.4 = (bf16[512,2048]{1,0:T(8,128)(2,1)S(1)}, bf16[512,2048]{1,0:T(8,128)(2,1)}, u32[]{:S(2)}) copy-start(bf16[512,2048]{1,0:T(8,128)(2,1)} %param.30) | copy-start | bytes 6291460
  67.0 0.7 copy-start.8
  67.0 1.1 copy-start.19
  71.2 60.6 %copy-start.9 = (f32[2048]{0:T(1024)S(1)}, f32[2048]{0:T(1024)}, u32[]{:S(2)}) copy-start(f32[2048]{0:T(1024)} %param.35) | copy-start | bytes 24580
  131.8 1.3 copy-start.2
  133.1 48.0 %copy-start.16 = (bf16[1,2048,512]{2,1,0:T(8,128)(2,1)S(1)}, bf16[1,2048,512]{2,1,0:T(8,128)(2,1)}, u32[]{:S(2)}) copy-start(bf16[1,2048,512]{2,1,0:T(8,128)(2,1)} %param.37) | copy-start | bytes 6291460
  179.4 1.7 copy-start.3
  192.2 5.8 %copy-start.7 = (bf16[2048,32]{0,1:T(8,128)(2,1)S(1)}, bf16[2048,32]{0,1:T(8,128)(2,1)}, u32[]{:S(2)}) copy-start(bf16[2048,32]{0,1:T(8,128)(2,1)} %param.36) | copy-start | bytes 393220
  192.2 45.8 %all-to-all-start.1 = ((bf16[32,24,2048]{2,1,0:T(8,128)(2,1)}), bf16[32,24,2048]{2,1,0:T(8,128)(2,1)}, u32[]{:S(2)}, u32[]{:S(2)}) async-start(bf16[32,24,2048]{2,1,0:T(8,128)(2,1)} %bitcast.175), calls=%async_computation.1 | async-start | bytes 6291456 | tf_op jit(solution)/shard_map/all_to_all | solution.py:151
  197.1 102.9 %reduce-scatter.2.cloned.1.call-start = ((), (), s32[]{:S(2)}) async-start(), calls=%async_computation.4 | async-start | bytes 1310720 | tf_op jit(solution)/shard_map/reduce_scatter | solution.py:155
  257.5 44.5 %copy-start.1 = (bf16[1,512,2048]{2,1,0:T(8,128)(2,1)S(1)}, bf16[1,512,2048]{2,1,0:T(8,128)(2,1)}, u32[]{:S(2)}) copy-start(bf16[1,512,2048]{2,1,0:T(8,128)(2,1)} %param.39) | copy-start | bytes 6291460
Sparse Core Ops, SparseCore 0:
  67.2 62.4 all-reduce.1
  267.6 32.3 reduce-scatter.1
where the time goes:
time: 314 us; the launch traced here: 309 us
  waiting for transfers between devices  123 us (39%)
  local copies, waits for them, and re-layouts  46.8 us (15%)
  blocking collectives  46.3 us (15%)
  matrix products  43.4 us (14%)
  other arithmetic  30 us (10%)
  between operations  14 us (4%)
  starting transfers between devices  4.99 us (2%)
    psum x1, waiting for transfers between devices, on_device(): summed_heads = lax.psum(partial_out, 'sec')  58.4 us
    all_to_all x1, blocking collectives, on_device(): lax.all_to_all(bucket, 'dp', split_axis=0, concat_axis=0, tiled=True)  46.3 us
    reduce_scatter x1, waiting for transfers between devices, on_device(): lax.psum_scatter(mixed_rows.astype(jnp.bfloat16), 'sec', scatter_dimensio...  32.5 us
    all_to_all x1, waiting for transfers between devices, on_device(): lax.all_to_all(partial_expert.astype(jnp.bfloat16), 'dp', split_axis=0, c...  32.5 us
    gather x2, local copies, waits for them, and re-layouts, on_device(): mixed_rows = jnp.sum(gate_values[:, :, None] * returned[slot_ids], axis=1)  14.1 us
    reduce_sum x1, other arithmetic, on_device(): mixed_rows = jnp.sum(gate_values[:, :, None] * returned[slot_ids], axis=1)  9.99 us
    dot_general x1, matrix products, on_device(): jnp.dot(activated, expert_down_weight[0], preferred_element_type=jnp.floa...  8.14 us
    dot_general x1, matrix products, on_device(): jnp.einsum('ubhd,ukhd->ubhk', query_rows, keys_hist, preferred_element_ty...  6.72 us
  transfers between devices with their start and end apart: 3, of which 3 were waited for; matrix products, arithmetic and copies ran while one was open for 4% of the time, Pallas kernels for 0%

commit v1 on v0

v1 whole, which is shorter than its diff:
```python
import functools
import math

import jax
import jax.numpy as jnp
from jax import lax
from jax.experimental import pallas as pl
from jax.experimental.pallas import tpu as pltpu
from jax.sharding import PartitionSpec as P

HD = 128
EPSILON = 1e-05
BF16 = jnp.bfloat16
F32 = jnp.float32
MIB = 1024 * 1024
WHOLE = pl.BlockSpec(memory_space=pltpu.VMEM)
IN_HBM = pl.BlockSpec(memory_space=pl.ANY)
IN_SMEM = pl.BlockSpec(memory_space=pltpu.SMEM)


def mm(a, b):
    return jnp.dot(a, b, preferred_element_type=F32)


def mm_nt(a, b):
    return lax.dot_general(a, b, (((1,), (1,)), ((), ())), preferred_element_type=F32)


def iota(shape, dim):
    return lax.broadcasted_iota(jnp.int32, shape, dim)


def call(kernel, out, in_specs, vmem_mib, flops, nbytes, scratch=(), transcendentals=0):
    return pl.pallas_call(
        kernel,
        out_shape=out,
        in_specs=in_specs,
        out_specs=jax.tree.map(lambda _: WHOLE, out),
        scratch_shapes=list(scratch),
        compiler_params=pltpu.CompilerParams(vmem_limit_bytes=vmem_mib * MIB),
        cost_estimate=pl.CostEstimate(
            flops=flops, bytes_accessed=nbytes, transcendentals=transcendentals
        ),
    )


def attention_kernel(
    kept, parent, gain, state_h, wq_h, wk_h, wv_h, wo_h, kh_h, vh_h, dk_h, dv_h,
    keep_own, keep_other, send,
    st, wq, wk, wv, wo, kh, vh, dk, dv, x, nrm, q, k, v, att, sems,
):
    users, slots, width = st.shape
    feat = wq.shape[1]
    heads = feat // HD
    sec = lax.axis_index("sec")
    z, c = sec // 2, sec % 2
    moves = {}

    def start(name, src, dst):
        copy = pltpu.make_async_copy(src, dst, sems.at[len(moves)])
        copy.start()
        moves[name] = copy

    start("st", state_h, st)
    start("wq", wq_h, wq)
    start("wk", wk_h, wk)
    start("wv", wv_h, wv)
    start("dk", dk_h, dk)
    start("dv", dv_h, dv)
    for u in range(users):
        start(("kh", u), kh_h.at[u], kh.at[u])
        start(("vh", u), vh_h.at[u], vh.at[u])
    start("wo", wo_h, wo)

    moves["st"].wait()
    for u in range(users):
        rows = pl.ds(u * slots, slots)
        pick = (iota((slots, slots), 0) == kept[u : u + 1, :]).astype(F32).T.astype(BF16)
        xu = mm(pick, st[u])
        x[rows, :] = xu
        mean = jnp.mean(xu * xu, axis=-1, keepdims=True)
        nrm[rows, :] = (xu * lax.rsqrt(mean + EPSILON) * gain[...]).astype(BF16)
    moves["wq"].wait()
    q[...] = mm(nrm[...], wq[...]).astype(BF16)
    moves["wk"].wait()
    k[...] = mm(nrm[...], wk[...]).astype(BF16)
    moves["wv"].wait()
    v[...] = mm(nrm[...], wv[...]).astype(BF16)
    moves["dk"].wait()
    moves["dv"].wait()

    scale = HD ** (-0.5) * math.log2(math.e)
    steps = dk.shape[1] // slots
    for u in range(users):
        rows = pl.ds(u * slots, slots)
        pk, pv = [], []
        for s in range(steps):
            hot = iota((steps * slots, slots), 0) == parent[u : u + 1, :] * steps + s
            pick = hot.astype(F32).T.astype(BF16)
            pk.append(mm(pick, dk[u]))
            pv.append(mm(pick, dv[u]))
        moves[("kh", u)].wait()
        moves[("vh", u)].wait()
        for h in range(heads):
            cols = slice(h * HD, (h + 1) * HD)
            qh = q[rows, cols]
            qf = qh.astype(F32)
            s_hist = mm_nt(qh, kh[u, :, cols])
            s_more = [jnp.sum(qf * p[:, cols], axis=-1, keepdims=True) for p in pk]
            s_more.append(jnp.sum(qf * k[rows, cols].astype(F32), axis=-1, keepdims=True))
            top = jnp.max(s_hist, axis=-1, keepdims=True)
            for s in s_more:
                top = jnp.maximum(top, s)
            e_hist = jnp.exp2((s_hist - top) * scale)
            mass = jnp.sum(e_hist, axis=-1, keepdims=True)
            mixed = mm(e_hist.astype(BF16), vh[u, :, cols])
            values = [p[:, cols] for p in pv] + [v[rows, cols].astype(F32)]
            for s, value in zip(s_more, values):
                e = jnp.exp2((s - top) * scale)
                mass = mass + e
                mixed = mixed + e * value
            att[rows, cols] = (mixed / mass).astype(BF16)

    moves["wo"].wait()

    def project(quarter):
        return mm(att[...], wo[:, pl.ds(pl.multiple_of(quarter * feat, feat), feat)])

    send[:, :feat] = project(2 * z + 1 - c).astype(BF16)
    send[:, feat:] = project(2 * (1 - z) + 1 - c).astype(BF16)
    keep_other[...] = project(2 * (1 - z) + c)
    keep_own[...] = project(sec) + x[:, pl.ds(pl.multiple_of(sec * feat, feat), feat)]


def routing_kernel(alive, choice, place, where):
    users, top, slots = choice.shape
    rows = users * slots
    lane = iota((1, slots), 1)
    live = jnp.concatenate([lane < alive[u] for u in range(users)], axis=1)
    experts = place.shape[0] // (6 * 8)
    earlier = (iota((rows, rows), 0) < iota((rows, rows), 1)).astype(F32).astype(BF16)
    base = jnp.zeros((experts, 1), F32)
    main, extra = [], []
    for t in range(top):
        e = jnp.concatenate([choice[u, t : t + 1, :] for u in range(users)], axis=1)
        hot = ((iota((experts, rows), 0) == e) & live).astype(F32)
        before = mm(hot.astype(BF16), earlier)
        rank = jnp.sum(hot * (before + base), axis=0, keepdims=True).astype(jnp.int32)
        base = base + jnp.sum(hot, axis=1, keepdims=True)
        over = rank - 16
        main.append(
            jnp.where(live & (rank < 16), (rank >> 3) * (experts * 8) + e * 8 + (rank & 7), -1)
        )
        extra.append(
            jnp.where(live & (rank >= 16), (over >> 2) * (experts * 8) + e * 8 + (over & 3), -8)
        )
    span = 2 * experts * 8
    index = iota((span, rows), 0)
    for part, (a, b) in enumerate(
        ((main[0], main[1]), (extra[0], extra[1]), (extra[0] + 4, extra[1] + 4))
    ):
        hit = (index == a) | (index == b)
        place[part * span : (part + 1) * span, :] = hit.astype(F32).astype(BF16)
    blank = jnp.zeros((4, rows), jnp.int32)
    where[...] = jnp.concatenate(main + extra + [blank], axis=0)


def dispatch_kernel(keep, from_core, from_z, gain, place, resid, message):
    feat = keep.shape[1]
    half = feat // 2
    span = place.shape[0] // 3
    sec = lax.axis_index("sec")
    r = keep[...] + from_core[:, :feat].astype(F32) + from_z[...].astype(F32)
    resid[...] = r
    scaled = (r * gain[:, pl.ds(pl.multiple_of(sec * feat, feat), feat)]).astype(BF16)
    main = mm(place[:span, :], scaled).astype(BF16)
    folded = mm(place[span : 2 * span, :], scaled[:, :half])
    folded = (folded + mm(place[2 * span :, :], scaled[:, half:])).astype(BF16)
    for z in range(2):
        message[z * span : (z + 1) * span, :feat] = main
        message[z * span : (z + 1) * span, feat:] = folded


def router_kernel(resid, gain, router, choice, part):
    users, top, slots = choice.shape
    rows = users * slots
    feat = resid.shape[1]
    experts = router.shape[0]
    sec = lax.axis_index("sec")
    cols = pl.ds(pl.multiple_of(sec * feat, feat), feat)
    r = resid[...]
    scaled = (r * gain[:, cols]).astype(BF16)
    logits = mm_nt(router[:, cols], scaled)
    out = []
    for t in range(top):
        e = jnp.concatenate([choice[u, t : t + 1, :] for u in range(users)], axis=1)
        hot = (iota((experts, rows), 0) == e).astype(F32)
        out.append(jnp.sum(hot * logits, axis=0, keepdims=True))
    squares = lax.dot_general(
        jnp.ones((8, feat), F32), r * r, (((1,), (1,)), ((), ())),
        precision=lax.Precision.HIGHEST, preferred_element_type=F32,
    )
    part[...] = jnp.concatenate(out + [squares[: 8 - top]], axis=0)


def gate_kernel(p0, p1, p2, p3, where, gates):
    rows = where.shape[1]
    total = (p0[...] + p1[...]) + (p2[...] + p3[...])
    width = gates.shape[1] // 3 * 4
    scale = lax.rsqrt(total[2:3] / width + EPSILON)
    sig = [1.0 / (1.0 + jnp.exp(-(total[t : t + 1] * scale))) for t in range(2)]
    weight = [s / (sig[0] + sig[1]) for s in sig]
    span = gates.shape[1] // 3
    index = iota((span, rows), 0)
    for part, shift in enumerate((0, 0, 4)):
        first = 0 if part == 0 else 2
        g = jnp.where(index == where[first : first + 1, :] + shift, weight[0], 0.0)
        g = jnp.where(index == where[first + 1 : first + 2, :] + shift, weight[1], g)
        gates[:, part * span : (part + 1) * span] = g.T.astype(BF16)


def fold_matrices(count):
    slot, place = iota((count * 4, count * 8), 0), iota((count * 4, count * 8), 1)
    at = (slot // 4) * 8 + slot % 4
    return [(place == at + shift).astype(F32) for shift in (0, 4)]


def expert_kernel(
    arrived, gain, wg0_h, wu0_h, wd0_h, wg1_h, wu1_h, wd1_h, message,
    wg0, wu0, wd0, wg1, wu1, wd1, x, act, sems,
):
    width, hidden = wg0.shape
    quarters = 4
    feat = width // quarters
    half = feat // 2
    block = arrived.shape[0] // quarters
    sources = block // 8
    copies = []
    for n, (src, dst) in enumerate(
        ((wg0_h, wg0), (wu0_h, wu0), (wg1_h, wg1), (wu1_h, wu1), (wd0_h, wd0), (wd1_h, wd1))
    ):
        copies.append(pltpu.make_async_copy(src.at[0], dst, sems.at[n]))
        copies[-1].start()
    folds = fold_matrices(sources)
    unfold = [f.astype(BF16) for f in folds]
    refold = [f.T.astype(BF16) for f in folds]
    for p in range(quarters):
        rows = slice(p * block, (p + 1) * block)
        x[:block, p * feat : (p + 1) * feat] = arrived[rows, :feat]
        tail = arrived[rows, feat:]
        for n in range(2):
            at = p * feat + n * half
            x[block:, at : at + half] = mm(unfold[n], tail).astype(BF16)
    plain = x[...].astype(F32) * (1.0 / gain[...])
    scale = lax.rsqrt(jnp.mean(plain * plain, axis=-1, keepdims=True) + EPSILON)
    for n, (wg, wu) in enumerate(((wg0, wu0), (wg1, wu1))):
        copies[2 * n].wait()
        g = mm(x[...], wg[...]) * scale
        copies[2 * n + 1].wait()
        u = mm(x[...], wu[...]) * scale
        act[:, n * hidden : (n + 1) * hidden] = (g / (1.0 + jnp.exp(-g)) * u).astype(BF16)
    copies[4].wait()
    copies[5].wait()
    for p in range(quarters):
        cols = slice(p * feat, (p + 1) * feat)
        rows = slice(p * block, (p + 1) * block)
        y = mm(act[:, :hidden], wd0[:, cols]) + mm(act[:, hidden:], wd1[:, cols])
        y = y.astype(BF16)
        message[rows, :feat] = y[:block]
        tail = mm(refold[0], y[block:, :half]) + mm(refold[1], y[block:, half:])
        message[rows, feat:] = tail.astype(BF16)


def combine_kernel(alive, resid, gates, arrived, out):
    users, slots, feat = out.shape
    half = feat // 2
    span = gates.shape[1] // 3
    main = jnp.zeros((users * slots, feat), F32)
    left = jnp.zeros((users * slots, half), F32)
    right = left
    for z in range(2):
        rows = slice(z * span, (z + 1) * span)
        tail = arrived[rows, feat:]
        main = main + mm(gates[:, :span], arrived[rows, :feat])
        left = left + mm(gates[:, span : 2 * span], tail)
        right = right + mm(gates[:, 2 * span :], tail)
    total = resid[...] + main + jnp.concatenate([left, right], axis=1)
    for u in range(users):
        live = iota((slots, feat), 0) < alive[u]
        rows = slice(u * slots, (u + 1) * slots)
        out[u] = jnp.where(live, total[rows], 0.0).astype(BF16)


def on_device(
    candidate_hidden_states,
    kept_candidate_index,
    slot_parent_beam,
    alive_slot_counts,
    slot_expert_index,
    attention_norm_gain,
    query_projection_weight,
    key_projection_weight,
    value_projection_weight,
    attention_output_weight,
    history_event_keys,
    history_event_values,
    decoded_beam_keys,
    decoded_beam_values,
    expert_norm_gain,
    router_projection_weight,
    expert_gate_weight,
    expert_up_weight,
    expert_down_weight,
):
    users, slots, width = candidate_hidden_states.shape
    feat = query_projection_weight.shape[1]
    history = history_event_keys.shape[1]
    steps = decoded_beam_keys.shape[2]
    experts = router_projection_weight.shape[1]
    hidden = expert_gate_weight.shape[2]
    rows = users * slots
    span = 2 * experts * 8
    core = [(s, s ^ 1) for s in range(4)]
    z_far = [(s, s ^ 2) for s in range(4)]
    both = [(s, s ^ 3) for s in range(4)]
    everyone = ("sec", "dp")
    struct = jax.ShapeDtypeStruct

    attention_gain = attention_norm_gain.reshape(1, width)
    expert_gain = expert_norm_gain.reshape(1, width)
    choice = jnp.swapaxes(slot_expert_index, 1, 2)
    router = router_projection_weight.T
    past_keys = decoded_beam_keys.reshape(users, slots * steps, feat)
    past_values = decoded_beam_values.reshape(users, slots * steps, feat)

    with jax.named_scope("attention"):
        keep_own, keep_other, send = call(
            attention_kernel,
            (struct((rows, feat), F32), struct((rows, feat), F32), struct((rows, 2 * feat), BF16)),
            [WHOLE] * 3 + [IN_HBM] * 9,
            50,
            3_300_000_000,
            20_000_000,
            [
                pltpu.VMEM((users, slots, width), BF16),
                pltpu.VMEM((width, feat), BF16),
                pltpu.VMEM((width, feat), BF16),
                pltpu.VMEM((width, feat), BF16),
                pltpu.VMEM((feat, width), BF16),
                pltpu.VMEM((users, history, feat), BF16),
                pltpu.VMEM((users, history, feat), BF16),
                pltpu.VMEM((users, slots * steps, feat), BF16),
                pltpu.VMEM((users, slots * steps, feat), BF16),
                pltpu.VMEM((rows, width), F32),
                pltpu.VMEM((rows, width), BF16),
                pltpu.VMEM((rows, feat), BF16),
                pltpu.VMEM((rows, feat), BF16),
                pltpu.VMEM((rows, feat), BF16),
                pltpu.VMEM((rows, feat), BF16),
                pltpu.SemaphoreType.DMA((7 + 2 * users,)),
            ],
            2_200_000,
        )(
            kept_candidate_index, slot_parent_beam, attention_gain, candidate_hidden_states,
            query_projection_weight, key_projection_weight, value_projection_weight,
            attention_output_weight, history_event_keys, history_event_values,
            past_keys, past_values,
        )
    with jax.named_scope("sibling_weights"):
        weights = [expert_gate_weight, expert_up_weight, expert_down_weight]
        sibling = [lax.ppermute(w, "sec", core) for w in weights]
    with jax.named_scope("head_sum"):
        from_core = lax.ppermute(send, "sec", core)
        to_z = (keep_other + from_core[:, feat:].astype(F32)).astype(BF16)
        from_z = lax.ppermute(to_z, "sec", z_far)
    with jax.named_scope("routing"):
        place, where = call(
            routing_kernel,
            (struct((3 * span, rows), BF16), struct((8, rows), jnp.int32)),
            [IN_SMEM, WHOLE],
            16,
            10_000_000,
            1_000_000,
        )(alive_slot_counts, choice)
    with jax.named_scope("dispatch"):
        resid, message = call(
            dispatch_kernel,
            (struct((rows, feat), F32), struct((2 * span, feat * 3 // 2), BF16)),
            [WHOLE] * 5,
            24,
            300_000_000,
            4_000_000,
        )(keep_own, from_core, from_z, expert_gain, place)
        arrived = lax.all_to_all(message, everyone, 0, 0, tiled=True)
    with jax.named_scope("router"):
        part = call(
            router_kernel,
            struct((8, rows), F32),
            [WHOLE] * 4,
            16,
            30_000_000,
            1_000_000,
        )(resid, expert_gain, router, choice)
        parts = [lax.ppermute(part, "sec", pairs) for pairs in (core, z_far, both)]
    with jax.named_scope("gates"):
        gates = call(
            gate_kernel,
            struct((rows, 3 * span), BF16),
            [WHOLE] * 5,
            16,
            3_000_000,
            1_000_000,
        )(part, *parts, where)
    with jax.named_scope("experts"):
        result = call(
            expert_kernel,
            struct((2 * span, feat * 3 // 2), BF16),
            [WHOLE] * 2 + [IN_HBM] * 6,
            50,
            4_800_000_000,
            16_000_000,
            [
                pltpu.VMEM((width, hidden), BF16),
                pltpu.VMEM((width, hidden), BF16),
                pltpu.VMEM((hidden, width), BF16),
                pltpu.VMEM((width, hidden), BF16),
                pltpu.VMEM((width, hidden), BF16),
                pltpu.VMEM((hidden, width), BF16),
                pltpu.VMEM((experts * 12, width), BF16),
                pltpu.VMEM((experts * 12, 2 * hidden), BF16),
                pltpu.SemaphoreType.DMA((6,)),
            ],
            400_000,
        )(arrived, expert_gain, *weights, *sibling)
        returned = lax.all_to_all(result, everyone, 0, 0, tiled=True)
    with jax.named_scope("combine"):
        return call(
            combine_kernel,
            struct((users, slots, feat), BF16),
            [IN_SMEM] + [WHOLE] * 3,
            24,
            600_000_000,
            4_000_000,
        )(alive_slot_counts, resid, gates, returned)


def solution(mesh):
    in_specs = (
        P("dp", None, None),
        P("dp", None),
        P("dp", None),
        P("dp"),
        P("dp", None, None),
        P(),
        P(None, "sec"),
        P(None, "sec"),
        P(None, "sec"),
        P("sec", None),
        P("dp", None, "sec"),
        P("dp", None, "sec"),
        P("dp", None, None, "sec"),
        P("dp", None, None, "sec"),
        P(),
        P(),
        P("dp", None, "sec"),
        P("dp", None, "sec"),
        P("dp", "sec", None),
    )
    out_specs = P("dp", None, "sec")
    return jax.shard_map(
        on_device, mesh=mesh, in_specs=in_specs, out_specs=out_specs, check_vma=False
    )
```

time: 314 us -> 104 us (0.33); the launches traced: 309 us -> 104 us
  waiting for transfers between devices: 123 us -> 50.9 us
  blocking collectives: 46.3 us -> 0 us
  matrix products: 43.4 us -> 0 us
  local copies, waits for them, and re-layouts: 46.8 us -> 4.89 us
  other arithmetic: 30 us -> 0.09 us
  Pallas kernels: 0 us -> 23.5 us
  starting transfers between devices: 4.99 us -> 24.2 us
  between operations: 14 us -> 0.19 us
    psum x1 -> x0, waiting for transfers between devices: 58.4 us -> none  [on_device(): summed_heads = lax.psum(partial_out, 'sec')]
    all_to_all x1 -> x0, blocking collectives: 46.3 us -> none  [on_device(): lax.all_to_all(bucket, 'dp', split_axis=0, concat_axis=0, tiled=True)]
    dot_general x12 -> x0, matrix products: 43.4 us -> none  [the longest x1 8.14 us: on_device(): jnp.dot(activated, expert_down_weight[0], preferred_element_type=jnp.floa...]
    reduce_scatter x1 -> x0, waiting for transfers between devices: 32.5 us -> none  [on_device(): lax.psum_scatter(mixed_rows.astype(jnp.bfloat16), 'sec', scatter_dimensio...]
    gather x12 -> x0, local copies, waits for them, and re-layouts: 31.5 us -> none  [the longest x2 14.1 us: on_device(): mixed_rows = jnp.sum(gate_values[:, :, None] * returned[slot_ids], axis=1)]
    pallas_call x0 -> x7, Pallas kernels: none -> 23.5 us  [the longest x1 9.69 us: on_device(): call(attention_kernel, (struct((rows, feat), F32), struct((rows, feat), F...]
    reduce_sum x7 -> x0, other arithmetic: 17 us -> none  [the longest x1 9.99 us: on_device(): mixed_rows = jnp.sum(gate_values[:, :, None] * returned[slot_ids], axis=1)]
    ppermute x0 -> x8, waiting for transfers between devices: none -> 10.8 us  [the longest x1 5.18 us: on_device(): from_z = lax.ppermute(to_z, 'sec', z_far)]
  transfers between devices with their start and end apart: 3 -> 10, of which waited for: 3 -> 6; matrix products, arithmetic and copies ran while one was open for 4% -> 0% of each run, Pallas kernels for 0% -> 3%
where the time goes in v1:
time: 104 us
  waiting for transfers between devices  50.9 us (49%)
  starting transfers between devices  24.2 us (23%)
  Pallas kernels  23.5 us (23%)
  local copies, waits for them, and re-layouts  4.89 us (5%)
    all_to_all x1, waiting for transfers between devices, on_device(): arrived = lax.all_to_all(message, everyone, 0, 0, tiled=True)  24.9 us
    all_to_all x1, waiting for transfers between devices, on_device(): returned = lax.all_to_all(result, everyone, 0, 0, tiled=True)  15.2 us
    all_to_all x1, starting transfers between devices, on_device(): arrived = lax.all_to_all(message, everyone, 0, 0, tiled=True)  10.2 us
    pallas_call x1, Pallas kernels, on_device(): call(attention_kernel, (struct((rows, feat), F32), struct((rows, feat), F...  9.69 us
    pallas_call x1, Pallas kernels, on_device(): call(expert_kernel, struct((2 * span, feat * 3 // 2), BF16), [WHOLE] * 2...  9.03 us
    ppermute x1, waiting for transfers between devices, on_device(): from_z = lax.ppermute(to_z, 'sec', z_far)  5.18 us
    ppermute x3, waiting for transfers between devices, on_device(): parts = [lax.ppermute(part, 'sec', pairs) for pairs in (core, z_far, both)]  4.71 us
    ppermute x3, starting transfers between devices, on_device(): parts = [lax.ppermute(part, 'sec', pairs) for pairs in (core, z_far, both)]  4.15 us
  transfers between devices with their start and end apart: 10, of which 6 were waited for; matrix products, arithmetic and copies ran while one was open for 0% of the time, Pallas kernels for 3%

profile of v1, /device:TPU:1, one launch (start us, length us, event | category | flops | bytes accessed | tf_op | source)
XLA Modules:
  0.0 103.8 jit_solution(3608826610871727693)
XLA Ops:
  0.0 1.3 %reshape.17.dk_h = bf16[2,256,512]{2,1,0:T(8,128)(2,1)S(1)} reshape(bf16[2,128,2,512]{3,2,1,0:T(2,128)(2,1)} %param.31) | data formatting | bytes 1048576 | tf_op jit(solution)/shard_map/reshape | solution.py:333
  1.4 1.2 %reshape.18.dv_h = bf16[2,256,512]{2,1,0:T(8,128)(2,1)S(1)} reshape(bf16[2,128,2,512]{3,2,1,0:T(2,128)(2,1)} %param.32) | data formatting | bytes 1048576 | tf_op jit(solution)/shard_map/reshape | solution.py:334
  2.6 0.0 copy-start.6
  2.6 0.0 copy-start.9
  2.7 0.0 copy-start.4
  2.7 9.7 %attention.1 = (f32[256,512]{1,0:T(8,128)S(1)}, f32[256,512]{1,0:T(8,128)S(1)}, bf16[256,1024]{1,0:T(8,128)(2,1)S(1)}) custom-call(s32[2,128]{1,0:T(2,128)S(1)} %copy-done.7, s32[2,128]{1,0:T(2,128)S(1)} %copy-done.8, f32[1,2048]{1,0:T(1,128)S(1)} %bitcast.16, bf16[2,128,2048]{2,1,0:T(8,128)(2,1)S(1)} %copy-done.2, bf16[2048,512]{1,0:T(8,128)(2,1)} %wq_h.1, ...), custom_call_target="tpu_custom_call" | custom-call | flops 3300000000 | bytes 20000000 | tf_op jit(solution)/shard_map/attention/pallas_call | solution.py:337
  12.4 1.5 %collective-permute-start = (bf16[256,1024]{1,0:T(8,128)(2,1)S(1)}, bf16[256,1024]{1,0:T(8,128)(2,1)S(1)}, u32[]{:S(2)}, u32[]{:S(2)}) collective-permute-start(bf16[256,1024]{1,0:T(8,128)(2,1)S(1)} %get-tuple-element.13), channel_id=1, source_target_pairs={{0,32},{32,0},{64,96},{96,64},{1,33},{33,1},{65,97},{97,65},{2,34}... | collective-permute-start | bytes 1572872 | tf_op jit(solution)/shard_map/head_sum/ppermute | solution.py:373
  13.9 0.1 collective-permute-start.5
  14.0 0.4 collective-permute-start.6
  14.4 0.1 collective-permute-start.7
  14.5 0.9 collective-permute-done.from_core
  15.4 0.1 add_convert_fusion
  15.5 3.8 %collective-permute-start.1 = (bf16[256,512]{1,0:T(8,128)(2,1)S(1)}, bf16[256,512]{1,0:T(8,128)(2,1)S(1)}, u32[]{:S(2)}, u32[]{:S(2)}) collective-permute-start(bf16[256,512]{1,0:T(8,128)(2,1)S(1)} %add_convert_fusion), channel_id=1, source_target_pairs={{0,64},{32,96},{64,0},{96,32},{1,65},{33,97},{65,1},{97,33},{2,66}... | collective-permute-start | bytes 786440 | tf_op jit(solution)/shard_map/head_sum/ppermute | solution.py:375
  19.3 1.2 %routing.1 = (bf16[1536,256]{1,0:T(8,128)(2,1)S(1)}, s32[8,256]{1,0:T(8,128)S(1)}) custom-call(s32[2]{0:T(128)S(1)} %copy-done.9, s32[2,2,128]{2,1,0:T(2,128)S(1)} %bitcast.17), custom_call_target="tpu_custom_call" | custom-call | flops 10000000 | bytes 1000000 | tf_op jit(solution)/shard_map/routing/pallas_call | solution.py:377
  20.5 5.2 %collective-permute-done.1.from_z = bf16[256,512]{1,0:T(8,128)(2,1)S(1)} collective-permute-done((bf16[256,512]{1,0:T(8,128)(2,1)S(1)}, bf16[256,512]{1,0:T(8,128)(2,1)S(1)}, u32[]{:S(2)}, u32[]{:S(2)}) %collective-permute-start.1) | collective-permute-done | bytes 262176 | tf_op jit(solution)/shard_map/head_sum/ppermute | solution.py:375
  25.6 0.5 dispatch.1
  26.2 1.1 %copy-done.1 = bf16[1024,768]{1,0:T(8,128)(2,1)} copy-done((bf16[1024,768]{1,0:T(8,128)(2,1)}, bf16[1024,768]{1,0:T(8,128)(2,1)S(1)}, u32[]{:S(2)}) %copy-start.1) | copy-done | bytes 1572888
  27.3 10.2 %all-to-all-start = ((bf16[128,8,768]{2,1,0:T(8,128)(2,1)}), bf16[128,8,768]{2,1,0:T(8,128)(2,1)S(1)}, u32[]{:S(2)}, u32[]{:S(2)}) async-start(bf16[128,8,768]{2,1,0:T(8,128)(2,1)} %bitcast.11), calls=%async_computation | async-start | bytes 3145728 | tf_op jit(solution)/shard_map/dispatch/all_to_all | solution.py:394
  37.6 0.0 collective-permute-done.6.wu1_h
  37.6 24.9 %all-to-all-done = bf16[128,8,768]{2,1,0:T(8,128)(2,1)S(1)} async-done(((bf16[128,8,768]{2,1,0:T(8,128)(2,1)}), bf16[128,8,768]{2,1,0:T(8,128)(2,1)S(1)}, u32[]{:S(2)}, u32[]{:S(2)}) %all-to-all-start) | async-done | bytes 1572896 | tf_op jit(solution)/shard_map/dispatch/all_to_all | solution.py:394
  62.5 9.0 %experts.1 = bf16[1024,768]{1,0:T(8,128)(2,1)S(1)} custom-call(bf16[1024,768]{1,0:T(8,128)(2,1)S(1)} %bitcast.10, f32[1,2048]{1,0:T(1,128)S(1)} %bitcast.14, bf16[1,2048,512]{2,1,0:T(8,128)(2,1)} %wg0_h.1, bf16[1,2048,512]{2,1,0:T(8,128)(2,1)} %wu0_h.1, bf16[1,512,2048]{2,1,0:T(8,128)(2,1)} %wd0_h.1, bf16[1,2048,512]{2,1,0:T(8,128)(2,1)} %collective-permute-done.5.wg1_h, ...), custom_call_target="tpu_custom_call" | custom-call | flops 4800000000 | bytes 16000000 | tf_op jit(solution)/shard_map/experts/pallas_call | solution.py:415
  71.6 1.1 %copy-done = bf16[1024,768]{1,0:T(8,128)(2,1)} copy-done((bf16[1024,768]{1,0:T(8,128)(2,1)}, bf16[1024,768]{1,0:T(8,128)(2,1)S(1)}, u32[]{:S(2)}) %copy-start) | copy-done | bytes 1572888
  72.7 4.0 %all-to-all-start.1 = ((bf16[128,8,768]{2,1,0:T(8,128)(2,1)}), bf16[128,8,768]{2,1,0:T(8,128)(2,1)S(1)}, u32[]{:S(2)}, u32[]{:S(2)}) async-start(bf16[128,8,768]{2,1,0:T(8,128)(2,1)} %bitcast.9), calls=%async_computation.1 | async-start | bytes 3145728 | tf_op jit(solution)/shard_map/experts/all_to_all | solution.py:435
  76.7 0.6 router.1.p0
  77.3 3.7 %collective-permute-start.4 = (f32[8,256]{1,0:T(8,128)S(1)}, f32[8,256]{1,0:T(8,128)S(1)}, u32[]{:S(2)}, u32[]{:S(2)}) collective-permute-start(f32[8,256]{1,0:T(8,128)S(1)} %router.1.p0), channel_id=1, source_target_pairs={{0,96},{32,64},{64,32},{96,0},{1,97},{33,65},{65,33},{97,1},{2,98}... | collective-permute-start | bytes 24584 | tf_op jit(solution)/shard_map/router/ppermute | solution.py:404
  81.0 0.4 collective-permute-start.3
  81.4 0.1 collective-permute-start.2
  81.5 1.4 %collective-permute-done.4.p3 = f32[8,256]{1,0:T(8,128)S(1)} collective-permute-done((f32[8,256]{1,0:T(8,128)S(1)}, f32[8,256]{1,0:T(8,128)S(1)}, u32[]{:S(2)}, u32[]{:S(2)}) %collective-permute-start.4) | collective-permute-done | bytes 8224 | tf_op jit(solution)/shard_map/router/ppermute | solution.py:404
  82.9 3.3 %collective-permute-done.3.p2 = f32[8,256]{1,0:T(8,128)S(1)} collective-permute-done((f32[8,256]{1,0:T(8,128)S(1)}, f32[8,256]{1,0:T(8,128)S(1)}, u32[]{:S(2)}, u32[]{:S(2)}) %collective-permute-start.3) | collective-permute-done | bytes 8224 | tf_op jit(solution)/shard_map/router/ppermute | solution.py:404
  86.2 0.5 gates.1
  86.7 15.2 %all-to-all-done.1 = bf16[128,8,768]{2,1,0:T(8,128)(2,1)S(1)} async-done(((bf16[128,8,768]{2,1,0:T(8,128)(2,1)}), bf16[128,8,768]{2,1,0:T(8,128)(2,1)S(1)}, u32[]{:S(2)}, u32[]{:S(2)}) %all-to-all-start.1) | async-done | bytes 1572896 | tf_op jit(solution)/shard_map/experts/all_to_all | solution.py:435
  101.8 2.0 %combine.1 = bf16[2,128,512]{2,1,0:T(8,128)(2,1)} custom-call(s32[2]{0:T(128)S(1)} %copy-done.9, f32[256,512]{1,0:T(8,128)S(1)} %get-tuple-element.16.resid, bf16[256,1536]{1,0:T(8,128)(2,1)S(1)} %gates.1, bf16[1024,768]{1,0:T(8,128)(2,1)S(1)} %bitcast.8), custom_call_target="tpu_custom_call" | custom-call | flops 600000000 | bytes 4000000 | tf_op jit(solution)/shard_map/combine/pallas_call | solution.py:437
  (18 shorter events, 0.0 us)
Async XLA Ops:
  0.0 2.6 %copy-start.5 = (f32[2048]{0:T(1024)S(1)}, f32[2048]{0:T(1024)}, u32[]{:S(2)}) copy-start(f32[2048]{0:T(1024)} %param.24) | copy-start | bytes 24580
  0.0 2.6 %copy-start.8 = (s32[2,128]{1,0:T(2,128)S(1)}, s32[2,128]{1,0:T(2,128)}, u32[]{:S(2)}) copy-start(s32[2,128]{1,0:T(2,128)} %parent.1) | copy-start | bytes 3076
  0.0 2.6 %copy-start.7 = (s32[2,128]{1,0:T(2,128)S(1)}, s32[2,128]{1,0:T(2,128)}, u32[]{:S(2)}) copy-start(s32[2,128]{1,0:T(2,128)} %kept.1) | copy-start | bytes 3076
  0.0 2.6 %copy-start.2 = (bf16[2,128,2048]{2,1,0:T(8,128)(2,1)S(1)}, bf16[2,128,2048]{2,1,0:T(8,128)(2,1)}, u32[]{:S(2)}) copy-start(bf16[2,128,2048]{2,1,0:T(8,128)(2,1)} %state_h.1) | copy-start | bytes 3145732
  2.6 16.6 %copy-start.6 = (s32[2,128,2]{1,2,0:T(2,128)S(1)}, s32[2,128,2]{1,2,0:T(2,128)}, u32[]{:S(2)}) copy-start(s32[2,128,2]{1,2,0:T(2,128)} %param.23) | copy-start | bytes 6148
  2.6 16.6 %copy-start.9 = (s32[2]{0:T(128)S(1)}, s32[2]{0:T(128)}, u32[]{:S(2)}) copy-start(s32[2]{0:T(128)} %alive.3) | copy-start | bytes 28
  2.7 23.0 %copy-start.4 = (f32[2048]{0:T(1024)S(1)}, f32[2048]{0:T(1024)}, u32[]{:S(2)}) copy-start(f32[2048]{0:T(1024)} %param.33) | copy-start | bytes 24580
  12.4 3.0 %collective-permute-start = (bf16[256,1024]{1,0:T(8,128)(2,1)S(1)}, bf16[256,1024]{1,0:T(8,128)(2,1)S(1)}, u32[]{:S(2)}, u32[]{:S(2)}) collective-permute-start(bf16[256,1024]{1,0:T(8,128)(2,1)S(1)} %get-tuple-element.13), channel_id=1, source_target_pairs={{0,32},{32,0},{64,96},{96,64},{1,33},{33,1},{65,97},{97,65},{2,34}... | collective-permute-start | bytes 1572872 | tf_op jit(solution)/shard_map/head_sum/ppermute | solution.py:373
  13.9 23.7 %collective-permute-start.5 = (bf16[1,2048,512]{2,1,0:T(8,128)(2,1)}, bf16[1,2048,512]{2,1,0:T(8,128)(2,1)}, u32[]{:S(2)}, u32[]{:S(2)}) collective-permute-start(bf16[1,2048,512]{2,1,0:T(8,128)(2,1)} %wg0_h.1), channel_id=1, source_target_pairs={{0,32},{32,0},{64,96},{96,64},{1,33},{33,1},{65,97},{97,65},{2,34}... | collective-permute-start | bytes 6291464 | tf_op jit(solution)/shard_map/sibling_weights/ppermute | solution.py:371
  14.0 23.6 %collective-permute-start.6 = (bf16[1,2048,512]{2,1,0:T(8,128)(2,1)}, bf16[1,2048,512]{2,1,0:T(8,128)(2,1)}, u32[]{:S(2)}, u32[]{:S(2)}) collective-permute-start(bf16[1,2048,512]{2,1,0:T(8,128)(2,1)} %wu0_h.1), channel_id=1, source_target_pairs={{0,32},{32,0},{64,96},{96,64},{1,33},{33,1},{65,97},{97,65},{2,34}... | collective-permute-start | bytes 6291464 | tf_op jit(solution)/shard_map/sibling_weights/ppermute | solution.py:371
  14.4 23.2 %collective-permute-start.7 = (bf16[1,512,2048]{2,1,0:T(8,128)(2,1)}, bf16[1,512,2048]{2,1,0:T(8,128)(2,1)}, u32[]{:S(2)}, u32[]{:S(2)}) collective-permute-start(bf16[1,512,2048]{2,1,0:T(8,128)(2,1)} %wd0_h.1), channel_id=1, source_target_pairs={{0,32},{32,0},{64,96},{96,64},{1,33},{33,1},{65,97},{97,65},{2,34}... | collective-permute-start | bytes 6291464 | tf_op jit(solution)/shard_map/sibling_weights/ppermute | solution.py:371
  15.5 10.1 %collective-permute-start.1 = (bf16[256,512]{1,0:T(8,128)(2,1)S(1)}, bf16[256,512]{1,0:T(8,128)(2,1)S(1)}, u32[]{:S(2)}, u32[]{:S(2)}) collective-permute-start(bf16[256,512]{1,0:T(8,128)(2,1)S(1)} %add_convert_fusion), channel_id=1, source_target_pairs={{0,64},{32,96},{64,0},{96,32},{1,65},{33,97},{65,1},{97,33},{2,66}... | collective-permute-start | bytes 786440 | tf_op jit(solution)/shard_map/head_sum/ppermute | solution.py:375
  26.2 1.1 %copy-start.1 = (bf16[1024,768]{1,0:T(8,128)(2,1)}, bf16[1024,768]{1,0:T(8,128)(2,1)S(1)}, u32[]{:S(2)}) copy-start(bf16[1024,768]{1,0:T(8,128)(2,1)S(1)} %get-tuple-element.18) | copy-start | bytes 4718596
  27.3 35.2 %all-to-all-start = ((bf16[128,8,768]{2,1,0:T(8,128)(2,1)}), bf16[128,8,768]{2,1,0:T(8,128)(2,1)S(1)}, u32[]{:S(2)}, u32[]{:S(2)}) async-start(bf16[128,8,768]{2,1,0:T(8,128)(2,1)} %bitcast.11), calls=%async_computation | async-start | bytes 3145728 | tf_op jit(solution)/shard_map/dispatch/all_to_all | solution.py:394
  71.6 1.2 %copy-start = (bf16[1024,768]{1,0:T(8,128)(2,1)}, bf16[1024,768]{1,0:T(8,128)(2,1)S(1)}, u32[]{:S(2)}) copy-start(bf16[1024,768]{1,0:T(8,128)(2,1)S(1)} %experts.1) | copy-start | bytes 4718596
  72.7 4.0 %copy-start.3 = (bf16[2048,32]{0,1:T(8,128)(2,1)S(1)}, bf16[2048,32]{0,1:T(8,128)(2,1)}, u32[]{:S(2)}) copy-start(bf16[2048,32]{0,1:T(8,128)(2,1)} %param.34) | copy-start | bytes 393220
  72.7 29.1 %all-to-all-start.1 = ((bf16[128,8,768]{2,1,0:T(8,128)(2,1)}), bf16[128,8,768]{2,1,0:T(8,128)(2,1)S(1)}, u32[]{:S(2)}, u32[]{:S(2)}) async-start(bf16[128,8,768]{2,1,0:T(8,128)(2,1)} %bitcast.9), calls=%async_computation.1 | async-start | bytes 3145728 | tf_op jit(solution)/shard_map/experts/all_to_all | solution.py:435
  77.3 5.6 %collective-permute-start.4 = (f32[8,256]{1,0:T(8,128)S(1)}, f32[8,256]{1,0:T(8,128)S(1)}, u32[]{:S(2)}, u32[]{:S(2)}) collective-permute-start(f32[8,256]{1,0:T(8,128)S(1)} %router.1.p0), channel_id=1, source_target_pairs={{0,96},{32,64},{64,32},{96,0},{1,97},{33,65},{65,33},{97,1},{2,98}... | collective-permute-start | bytes 24584 | tf_op jit(solution)/shard_map/router/ppermute | solution.py:404
  81.0 5.2 %collective-permute-start.3 = (f32[8,256]{1,0:T(8,128)S(1)}, f32[8,256]{1,0:T(8,128)S(1)}, u32[]{:S(2)}, u32[]{:S(2)}) collective-permute-start(f32[8,256]{1,0:T(8,128)S(1)} %router.1.p0), channel_id=1, source_target_pairs={{0,64},{32,96},{64,0},{96,32},{1,65},{33,97},{65,1},{97,33},{2,66}... | collective-permute-start | bytes 24584 | tf_op jit(solution)/shard_map/router/ppermute | solution.py:404
  81.4 4.8 %collective-permute-start.2 = (f32[8,256]{1,0:T(8,128)S(1)}, f32[8,256]{1,0:T(8,128)S(1)}, u32[]{:S(2)}, u32[]{:S(2)}) collective-permute-start(f32[8,256]{1,0:T(8,128)S(1)} %router.1.p0), channel_id=1, source_target_pairs={{0,32},{32,0},{64,96},{96,64},{1,33},{33,1},{65,97},{97,65},{2,34}... | collective-permute-start | bytes 24584 | tf_op jit(solution)/shard_map/router/ppermute | solution.py:404

commit v2 on v1

v2 whole, which is shorter than its diff:
```python
import functools
import math

import jax
import jax.numpy as jnp
from jax import lax
from jax.experimental import pallas as pl
from jax.experimental.pallas import tpu as pltpu
from jax.sharding import PartitionSpec as P

HD = 128
EPSILON = 1e-05
BF16 = jnp.bfloat16
F32 = jnp.float32
MIB = 1024 * 1024
WHOLE = pl.BlockSpec(memory_space=pltpu.VMEM)
IN_HBM = pl.BlockSpec(memory_space=pl.ANY)
IN_SMEM = pl.BlockSpec(memory_space=pltpu.SMEM)


def mm(a, b):
    return jnp.dot(a, b, preferred_element_type=F32)


def mm_nt(a, b):
    return lax.dot_general(a, b, (((1,), (1,)), ((), ())), preferred_element_type=F32)


def iota(shape, dim):
    return lax.broadcasted_iota(jnp.int32, shape, dim)


def call(kernel, out, in_specs, vmem_mib, flops, nbytes, scratch=(), transcendentals=0, out_specs=None):
    return pl.pallas_call(
        kernel,
        out_shape=out,
        in_specs=in_specs,
        out_specs=jax.tree.map(lambda _: WHOLE, out) if out_specs is None else out_specs,
        scratch_shapes=list(scratch),
        compiler_params=pltpu.CompilerParams(vmem_limit_bytes=vmem_mib * MIB),
        cost_estimate=pl.CostEstimate(
            flops=flops, bytes_accessed=nbytes, transcendentals=transcendentals
        ),
    )


class Loads:
    def __init__(self, sems):
        self.sems = sems
        self.copies, self.count = {}, 0

    def start(self, name, *pieces):
        for src, dst in pieces:
            copy = pltpu.make_async_copy(src, dst, self.sems.at[self.count])
            copy.start()
            self.copies.setdefault(name, []).append(copy)
            self.count += 1

    def start_rows(self, name, src, dst, pieces):
        size = dst.shape[0] // pieces
        cuts = [pl.ds(n * size, size) for n in range(pieces)]
        self.start(name, *[(src.at[cut], dst.at[cut]) for cut in cuts])

    def wait(self, name):
        for copy in self.copies[name]:
            copy.wait()


def attention_kernel(
    kept_h, parent_h, gain_h, state_h, wq_h, wk_h, wv_h, wo_h, kh_h, vh_h, dk_h, dv_h,
    keep_own, keep_other, send,
    kept, parent, gain, st, sq, wq, wk, wv, wo, kh, vh, dk, dv, nrm, q, k, v, own, att, scores, sems,
):
    users, slots, width = st.shape
    history = kh.shape[1]
    feat = wq.shape[1]
    heads = feat // HD
    sec = lax.axis_index("sec")
    z, c = sec // 2, sec % 2

    def quarter(n):
        return pl.ds(pl.multiple_of(n * feat, feat), feat)

    order = (sec, 2 * (1 - z) + c, 2 * z + 1 - c, 2 * (1 - z) + 1 - c)
    loads = Loads(sems)
    loads.start("small", (kept_h, kept), (parent_h, parent), (gain_h, gain))
    for u in range(users):
        loads.start_rows(("st", u), state_h.at[u], st.at[u], 2)
    loads.start_rows("wq", wq_h, wq, 4)
    loads.start_rows("wk", wk_h, wk, 4)
    loads.start_rows("wv", wv_h, wv, 4)
    for u in range(users):
        loads.start(
            ("past", u),
            (dk_h.at[u].reshape(dk.shape[1:]), dk.at[u]),
            (dv_h.at[u].reshape(dv.shape[1:]), dv.at[u]),
        )
        loads.start_rows(("kh", u), kh_h.at[u], kh.at[u], 4)
        loads.start_rows(("vh", u), vh_h.at[u], vh.at[u], 4)
    loads.start("sq", (state_h.at[:, :, quarter(sec)], sq))
    loads.start("wo", *[
        (wo_h.at[:, quarter(n)], wo.at[:, pl.ds(at * feat, feat)]) for at, n in enumerate(order)
    ])

    loads.wait("small")
    picks = []
    for u in range(users):
        rows = pl.ds(u * slots, slots)
        picks.append((iota((slots, slots), 0) == kept[u : u + 1, :]).astype(F32).T.astype(BF16))
        loads.wait(("st", u))
        xu = mm(picks[u], st[u])
        mean = jnp.mean(xu * xu, axis=-1, keepdims=True)
        nrm[rows, :] = (xu * lax.rsqrt(mean + EPSILON) * gain[...]).astype(BF16)
    loads.wait("wq")
    q[...] = mm(nrm[...], wq[...]).astype(BF16)
    loads.wait("wk")
    k[...] = mm(nrm[...], wk[...]).astype(BF16)
    loads.wait("wv")
    v[...] = mm(nrm[...], wv[...]).astype(BF16)

    scale = HD ** (-0.5) * math.log2(math.e)
    steps = dk.shape[1] // slots
    chunk = 512
    chunks = [slice(a, a + chunk) for a in range(0, history, chunk)]
    group = 2
    tall, wide = group * slots, group * HD
    sets = [(u, h) for u in range(users) for h in range(0, heads, group)]
    past = {}
    ready = {}

    def stack(f):
        return jnp.concatenate([f(slice(m * HD, (m + 1) * HD)) for m in range(group)], axis=0)

    for n in range(len(sets) + 1):
        if n < len(sets):
            u, h = sets[n]
            rows = pl.ds(u * slots, slots)
            cols = slice(h * HD, h * HD + wide)
            if h == 0:
                loads.wait(("past", u))
                past[u] = []
                for s in range(steps):
                    hot = iota((steps * slots, slots), 0) == parent[u : u + 1, :] * steps + s
                    pick = hot.astype(F32).T.astype(BF16)
                    past[u].append((mm(pick, dk[u]), mm(pick, dv[u])))
                loads.wait(("kh", u))
                loads.wait(("vh", u))
            qs = q[rows, cols]
            blank = jnp.zeros((slots, HD), BF16)
            diagonal = jnp.concatenate(
                [
                    jnp.concatenate(
                        [qs[:, m * HD : (m + 1) * HD] if m == at else blank for m in range(group)], axis=1
                    )
                    for at in range(group)
                ],
                axis=0,
            )
            qf = qs.astype(F32)
            more = []
            for p in [p for p, _ in past[u]] + [k[rows, :].astype(F32)]:
                both = qf * p[:, cols]
                more.append(stack(lambda m: jnp.sum(both[:, m], axis=-1, keepdims=True)))
            high = jnp.full((tall, HD), -jnp.inf, F32)
        if n > 0:
            u0, h0, more0, top = ready.pop(n - 1)
            rows0 = pl.ds(u0 * slots, slots)
            cols0 = slice(h0 * HD, h0 * HD + wide)
            mass = jnp.zeros((tall, HD), F32)
            mixed = jnp.zeros((tall, wide), F32)
        for at in chunks:
            if n < len(sets):
                s = mm_nt(diagonal, kh[u, at, cols])
                scores[n % 2, :, at] = s
                for a in range(0, chunk, HD):
                    high = jnp.maximum(high, s[:, a : a + HD])
            if n > 0:
                e = jnp.exp2((scores[(n - 1) % 2, :, at] - top) * scale)
                for a in range(0, chunk, HD):
                    mass = mass + e[:, a : a + HD]
                mixed = mixed + mm(e.astype(BF16), vh[u0, at, cols0])
        if n < len(sets):
            peak = jnp.max(high, axis=-1, keepdims=True)
            for s in more:
                peak = jnp.maximum(peak, s)
            ready[n] = (u, h, more, peak)
        if n > 0:
            total = jnp.sum(mass, axis=-1, keepdims=True)
            mixed = jnp.concatenate(
                [mixed[m * slots : (m + 1) * slots, m * HD : (m + 1) * HD] for m in range(group)], axis=0
            )
            values = [p[:, cols0] for _, p in past[u0]] + [v[rows0, cols0].astype(F32)]
            for s, value in zip(more0, values):
                e = jnp.exp2((s - top) * scale)
                total = total + e
                mixed = mixed + e * stack(lambda m: value[:, m])
            mixed = (mixed / total).astype(BF16)
            att[rows0, cols0] = jnp.concatenate(
                [mixed[m * slots : (m + 1) * slots] for m in range(group)], axis=1
            )

    loads.wait("sq")
    for u in range(users):
        own[pl.ds(u * slots, slots), :] = mm(picks[u], sq[u]).astype(BF16)
    loads.wait("wo")
    out = mm(att[...], wo[...])
    keep_own[...] = out[:, :feat] + own[...].astype(F32)
    keep_other[...] = out[:, feat : 2 * feat]
    send[...] = out[:, 2 * feat :].astype(BF16)


def routing_kernel(alive, choice, place, where):
    users, top, slots = choice.shape
    rows = users * slots
    lane = iota((1, slots), 1)
    live = jnp.concatenate([lane < alive[u] for u in range(users)], axis=1)
    experts = place.shape[0] // (6 * 8)
    earlier = (iota((rows, rows), 0) < iota((rows, rows), 1)).astype(F32).astype(BF16)
    base = jnp.zeros((experts, 1), F32)
    main, extra = [], []
    for t in range(top):
        e = jnp.concatenate([choice[u, t : t + 1, :] for u in range(users)], axis=1)
        hot = ((iota((experts, rows), 0) == e) & live).astype(F32)
        before = mm(hot.astype(BF16), earlier)
        rank = jnp.sum(hot * (before + base), axis=0, keepdims=True).astype(jnp.int32)
        base = base + jnp.sum(hot, axis=1, keepdims=True)
        over = rank - 16
        main.append(
            jnp.where(live & (rank < 16), (rank >> 3) * (experts * 8) + e * 8 + (rank & 7), -1)
        )
        extra.append(
            jnp.where(live & (rank >= 16), (over >> 2) * (experts * 8) + e * 8 + (over & 3), -8)
        )
    span = 2 * experts * 8
    index = iota((span, rows), 0)
    for part, (a, b) in enumerate(
        ((main[0], main[1]), (extra[0], extra[1]), (extra[0] + 4, extra[1] + 4))
    ):
        hit = (index == a) | (index == b)
        place[part * span : (part + 1) * span, :] = hit.astype(F32).astype(BF16)
    blank = jnp.zeros((4, rows), jnp.int32)
    where[...] = jnp.concatenate(main + extra + [blank], axis=0)


def dispatch_kernel(keep, from_core, from_z, gain, place, resid, message, block, sems):
    feat = keep.shape[1]
    half = feat // 2
    span = place.shape[0] // 3
    part = span // 2
    sec = lax.axis_index("sec")
    r = keep[...] + from_core[:, :feat].astype(F32) + from_z[...].astype(F32)
    scaled = (r * gain[:, pl.ds(pl.multiple_of(sec * feat, feat), feat)]).astype(BF16)
    copies = []
    for n in range(2):
        rows = slice(n * part, (n + 1) * part)
        block[rows, :feat] = mm(place[rows, :], scaled).astype(BF16)
        folded = mm(place[span + n * part : span + (n + 1) * part, :], scaled[:, :half])
        folded = folded + mm(
            place[2 * span + n * part : 2 * span + (n + 1) * part, :], scaled[:, half:]
        )
        block[rows, feat:] = folded.astype(BF16)
        for z in range(2):
            copies.append(
                pltpu.make_async_copy(
                    block.at[pl.ds(n * part, part)],
                    message.at[pl.ds(z * span + n * part, part)],
                    sems.at[len(copies)],
                )
            )
            copies[-1].start()
    resid[...] = r
    for copy in copies:
        copy.wait()


def router_kernel(resid, gain, router, choice, part):
    users, top, slots = choice.shape
    rows = users * slots
    feat = resid.shape[1]
    experts = router.shape[0]
    sec = lax.axis_index("sec")
    cols = pl.ds(pl.multiple_of(sec * feat, feat), feat)
    r = resid[...]
    scaled = (r * gain[:, cols]).astype(BF16)
    logits = mm_nt(router[:, cols], scaled)
    out = []
    for t in range(top):
        e = jnp.concatenate([choice[u, t : t + 1, :] for u in range(users)], axis=1)
        hot = (iota((experts, rows), 0) == e).astype(F32)
        out.append(jnp.sum(hot * logits, axis=0, keepdims=True))
    squares = lax.dot_general(
        jnp.ones((8, feat), F32), r * r, (((1,), (1,)), ((), ())),
        precision=lax.Precision.HIGHEST, preferred_element_type=F32,
    )
    part[...] = jnp.concatenate(out + [squares[: 8 - top]], axis=0)


def gate_kernel(p0, p1, p2, p3, where, gates):
    rows = where.shape[1]
    total = (p0[...] + p1[...]) + (p2[...] + p3[...])
    width = gates.shape[1] // 3 * 4
    scale = lax.rsqrt(total[2:3] / width + EPSILON)
    sig = [1.0 / (1.0 + jnp.exp(-(total[t : t + 1] * scale))) for t in range(2)]
    weight = [s / (sig[0] + sig[1]) for s in sig]
    span = gates.shape[1] // 3
    index = iota((span, rows), 0)
    for part, shift in enumerate((0, 0, 4)):
        first = 0 if part == 0 else 2
        g = jnp.where(index == where[first : first + 1, :] + shift, weight[0], 0.0)
        g = jnp.where(index == where[first + 1 : first + 2, :] + shift, weight[1], g)
        gates[:, part * span : (part + 1) * span] = g.T.astype(BF16)


def unfold(folded):
    rows, width = folded.shape
    pair = folded.astype(F32).reshape(rows // 16, 2, 8, width)
    a, b = pair[:, 0], pair[:, 1]
    first = iota(a.shape, 1) < 4
    left = jnp.where(first, a, pltpu.roll(b, 4, 1))
    right = jnp.where(first, pltpu.roll(a, 4, 1), b)
    return [t.reshape(rows // 2, width).astype(BF16) for t in (left, right)]


def fold(left, right):
    rows, width = left.shape
    left, right = (t.reshape(rows // 8, 8, width) for t in (left, right))
    first = iota(left.shape, 1) < 4
    a = jnp.where(first, left, pltpu.roll(right, 4, 1))
    b = jnp.where(first, pltpu.roll(left, 4, 1), right)
    return jnp.stack([a, b], axis=1).reshape(rows * 2, width)


def expert_kernel(
    arrived, gain, wg0_h, wu0_h, wd0_h, wg1_h, wu1_h, wd1_h, message,
    wg0, wu0, wg1, wu1, wd, x, act, block, sems, out_sems,
):
    width, hidden = wg0.shape
    quarters = 4
    feat = width // quarters
    half = feat // 2
    part = arrived.shape[0] // quarters
    loads = Loads(sems)
    for n, (src, dst) in enumerate(((wg0_h, wg0), (wu0_h, wu0), (wg1_h, wg1), (wu1_h, wu1))):
        loads.start_rows(n, src.at[0], dst, 4)
    loads.start_rows(4, wd0_h.at[0], wd.at[pl.ds(0, hidden)], 4)
    loads.start_rows(5, wd1_h.at[0], wd.at[pl.ds(hidden, hidden)], 4)
    for p in range(quarters):
        rows = slice(p * part, (p + 1) * part)
        x[:part, p * feat : (p + 1) * feat] = arrived[rows, :feat]
        for n, piece in enumerate(unfold(arrived[rows, feat:])):
            at = p * feat + n * half
            x[part:, at : at + half] = piece
    plain = x[...].astype(F32) * (1.0 / gain[...])
    scale = lax.rsqrt(jnp.mean(plain * plain, axis=-1, keepdims=True) + EPSILON)
    for n, (wg, wu) in enumerate(((wg0, wu0), (wg1, wu1))):
        loads.wait(2 * n)
        g = mm(x[...], wg[...]) * scale
        loads.wait(2 * n + 1)
        u = mm(x[...], wu[...]) * scale
        act[:, n * hidden : (n + 1) * hidden] = (g / (1.0 + jnp.exp(-g)) * u).astype(BF16)
    loads.wait(4)
    loads.wait(5)
    copies = []
    for p in range(quarters):
        cols = slice(p * feat, (p + 1) * feat)
        rows = slice(p * part, (p + 1) * part)
        y = mm(act[...], wd[:, cols])
        block[rows, :feat] = y[:part].astype(BF16)
        block[rows, feat:] = fold(y[part:, :half], y[part:, half:]).astype(BF16)
        for n in range(4):
            here = pl.ds(p * part + n * (part // 4), part // 4)
            copies.append(
                pltpu.make_async_copy(block.at[here], message.at[here], out_sems.at[len(copies)])
            )
            copies[-1].start()
    for copy in copies:
        copy.wait()


def combine_kernel(alive, resid, gates, arrived, out):
    users, slots, feat = out.shape
    span = gates.shape[1] // 3

    def bring(part, cols):
        g = gates[:, part * span : (part + 1) * span]
        return mm(jnp.concatenate([g, g], axis=1), arrived[:, cols])

    main = bring(0, slice(0, feat))
    tail = slice(feat, arrived.shape[1])
    total = resid[...] + main + jnp.concatenate([bring(1, tail), bring(2, tail)], axis=1)
    for u in range(users):
        live = iota((slots, feat), 0) < alive[u]
        rows = slice(u * slots, (u + 1) * slots)
        out[u] = jnp.where(live, total[rows], 0.0).astype(BF16)


struct = jax.ShapeDtypeStruct


def in_hbm(a):
    return pltpu.with_memory_space_constraint(a, pltpu.HBM)


def attention(kept, parent, gain, state, wq, wk, wv, wo, keys, values, past_keys, past_values):
    users, slots, width = state.shape
    feat = wq.shape[1]
    history = keys.shape[1]
    steps = past_keys.shape[2]
    rows = users * slots
    return call(
        attention_kernel,
        (struct((rows, feat), F32), struct((rows, feat), F32), struct((rows, 2 * feat), BF16)),
        [IN_HBM] * 12,
        40,
        3_300_000_000,
        20_000_000,
        [
            pltpu.VMEM(kept.shape, jnp.int32),
            pltpu.VMEM(parent.shape, jnp.int32),
            pltpu.VMEM(gain.shape, F32),
            pltpu.VMEM((users, slots, width), BF16),
            pltpu.VMEM((users, slots, feat), BF16),
            pltpu.VMEM((width, feat), BF16),
            pltpu.VMEM((width, feat), BF16),
            pltpu.VMEM((width, feat), BF16),
            pltpu.VMEM((feat, width), BF16),
            pltpu.VMEM((users, history, feat), BF16),
            pltpu.VMEM((users, history, feat), BF16),
            pltpu.VMEM((users, slots * steps, feat), BF16),
            pltpu.VMEM((users, slots * steps, feat), BF16),
            pltpu.VMEM((rows, width), BF16),
            pltpu.VMEM((rows, feat), BF16),
            pltpu.VMEM((rows, feat), BF16),
            pltpu.VMEM((rows, feat), BF16),
            pltpu.VMEM((rows, feat), BF16),
            pltpu.VMEM((rows, feat), BF16),
            pltpu.VMEM((2, 2 * slots, history), F32),
            pltpu.SemaphoreType.DMA((20 + 12 * users,)),
        ],
        2_200_000,
    )(
        *[
            in_hbm(a)
            for a in (
                kept, parent, gain, state, wq, wk, wv, wo, keys, values, past_keys, past_values,
            )
        ]
    )


def route(alive, choice, experts):
    users, top, slots = choice.shape
    rows = users * slots
    return call(
        routing_kernel,
        (struct((6 * 8 * experts, rows), BF16), struct((8, rows), jnp.int32)),
        [IN_SMEM, WHOLE],
        16,
        10_000_000,
        1_000_000,
    )(alive, choice)


def dispatch(keep, from_core, from_z, gain, place):
    rows, feat = keep.shape
    span = place.shape[0] // 3
    return call(
        dispatch_kernel,
        (struct((rows, feat), F32), pltpu.HBM((2 * span, feat * 3 // 2), BF16)),
        [WHOLE] * 5,
        16,
        300_000_000,
        4_000_000,
        [pltpu.VMEM((span, feat * 3 // 2), BF16), pltpu.SemaphoreType.DMA((4,))],
        out_specs=(WHOLE, IN_HBM),
    )(keep, from_core, from_z, gain, place)


def chosen_logits(resid, gain, router, choice):
    return call(
        router_kernel, struct((8, resid.shape[0]), F32), [WHOLE] * 4, 16, 30_000_000, 1_000_000
    )(resid, gain, router, choice)


def gate_matrix(parts, where, experts):
    return call(
        gate_kernel,
        struct((where.shape[1], 6 * 8 * experts), BF16),
        [WHOLE] * 5,
        16,
        3_000_000,
        1_000_000,
    )(*parts, where)


def run_expert(arrived, gain, weights):
    _, width, hidden = weights[0].shape
    rows = arrived.shape[0] // 8 * 3
    return call(
        expert_kernel,
        pltpu.HBM(arrived.shape, BF16),
        [WHOLE] * 2 + [IN_HBM] * 6,
        40,
        4_800_000_000,
        16_000_000,
        [
            pltpu.VMEM((width, hidden), BF16),
            pltpu.VMEM((width, hidden), BF16),
            pltpu.VMEM((width, hidden), BF16),
            pltpu.VMEM((width, hidden), BF16),
            pltpu.VMEM((2 * hidden, width), BF16),
            pltpu.VMEM((rows, width), BF16),
            pltpu.VMEM((rows, 2 * hidden), BF16),
            pltpu.VMEM(arrived.shape, BF16),
            pltpu.SemaphoreType.DMA((24,)),
            pltpu.SemaphoreType.DMA((16,)),
        ],
        400_000,
        IN_HBM,
    )(arrived, gain, *[in_hbm(w) for w in weights])


def combine(alive, resid, gates, returned, users):
    rows, feat = resid.shape
    return call(
        combine_kernel,
        struct((users, rows // users, feat), BF16),
        [IN_SMEM] + [WHOLE] * 3,
        24,
        600_000_000,
        4_000_000,
    )(alive, resid, gates, returned)


def on_device(
    candidate_hidden_states,
    kept_candidate_index,
    slot_parent_beam,
    alive_slot_counts,
    slot_expert_index,
    attention_norm_gain,
    query_projection_weight,
    key_projection_weight,
    value_projection_weight,
    attention_output_weight,
    history_event_keys,
    history_event_values,
    decoded_beam_keys,
    decoded_beam_values,
    expert_norm_gain,
    router_projection_weight,
    expert_gate_weight,
    expert_up_weight,
    expert_down_weight,
):
    users, slots, width = candidate_hidden_states.shape
    feat = query_projection_weight.shape[1]
    experts = router_projection_weight.shape[1]
    core = [(s, s ^ 1) for s in range(4)]
    z_far = [(s, s ^ 2) for s in range(4)]
    both = [(s, s ^ 3) for s in range(4)]
    everyone = ("sec", "dp")

    attention_gain = attention_norm_gain.reshape(1, width)
    expert_gain = expert_norm_gain.reshape(1, width)
    choice = jnp.swapaxes(slot_expert_index, 1, 2)
    router = router_projection_weight.T

    with jax.named_scope("attention"):
        keep_own, keep_other, send = attention(
            kept_candidate_index, slot_parent_beam, attention_gain, candidate_hidden_states,
            query_projection_weight, key_projection_weight, value_projection_weight,
            attention_output_weight, history_event_keys, history_event_values,
            decoded_beam_keys, decoded_beam_values,
        )
    with jax.named_scope("head_sum"):
        from_core = lax.ppermute(send, "sec", core)
        to_z = (keep_other + from_core[:, feat:].astype(F32)).astype(BF16)
        from_z = lax.ppermute(to_z, "sec", z_far)
    with jax.named_scope("routing"):
        place, where = route(alive_slot_counts, choice, experts)
    with jax.named_scope("sibling_weights"):
        weights = [expert_gate_weight, expert_up_weight, expert_down_weight]
        late = lax.optimization_barrier((*weights, where))[:3]
        weights = weights + [lax.ppermute(w, "sec", core) for w in late]
    with jax.named_scope("dispatch"):
        resid, message = dispatch(keep_own, from_core, from_z, expert_gain, place)
        arrived = lax.all_to_all(message, everyone, 0, 0, tiled=True)
    with jax.named_scope("router"):
        part = chosen_logits(resid, expert_gain, router, choice)
        parts = [part] + [lax.ppermute(part, "sec", pairs) for pairs in (core, z_far, both)]
    with jax.named_scope("gates"):
        gates = gate_matrix(parts, where, experts)
    with jax.named_scope("experts"):
        result = run_expert(arrived, expert_gain, weights)
        returned = lax.all_to_all(result, everyone, 0, 0, tiled=True)
    with jax.named_scope("combine"):
        return combine(alive_slot_counts, resid, gates, returned, users)


def solution(mesh):
    in_specs = (
        P("dp", None, None),
        P("dp", None),
        P("dp", None),
        P("dp"),
        P("dp", None, None),
        P(),
        P(None, "sec"),
        P(None, "sec"),
        P(None, "sec"),
        P("sec", None),
        P("dp", None, "sec"),
        P("dp", None, "sec"),
        P("dp", None, None, "sec"),
        P("dp", None, None, "sec"),
        P(),
        P(),
        P("dp", None, "sec"),
        P("dp", None, "sec"),
        P("dp", "sec", None),
    )
    out_specs = P("dp", None, "sec")
    return jax.shard_map(
        on_device, mesh=mesh, in_specs=in_specs, out_specs=out_specs, check_vma=False
    )
```

time: 104 us -> 100 us (0.962)
  local copies, waits for them, and re-layouts: 4.89 us -> 0.02 us
    reshape x2 -> x0, local copies, waits for them, and re-layouts: 2.57 us -> none  [the longest x1 1.33 us: on_device(): past_keys = decoded_beam_keys.reshape(users, slots * steps, feat)]
    unnamed x20 -> x8, local copies, waits for them, and re-layouts: 2.32 us -> 0.02 us
    ppermute x1, waiting for transfers between devices: 5.18 us -> 6.33 us  [on_device(): from_z = lax.ppermute(to_z, 'sec', z_far)]
  transfers between devices with their start and end apart: 10 -> 10, of which waited for: 6 -> 5; matrix products, arithmetic and copies ran while one was open for 0% -> 0% of each run, Pallas kernels for 3% -> 4%
where the time goes in v2:
time: 100 us
  waiting for transfers between devices  51.2 us (51%)
  starting transfers between devices  24.4 us (24%)
  Pallas kernels  24.3 us (24%)
    all_to_all x1, waiting for transfers between devices, on_device(): arrived = lax.all_to_all(message, everyone, 0, 0, tiled=True)  24.9 us
    all_to_all x1, waiting for transfers between devices, on_device(): returned = lax.all_to_all(result, everyone, 0, 0, tiled=True)  15.2 us
    all_to_all x1, starting transfers between devices, on_device(): arrived = lax.all_to_all(message, everyone, 0, 0, tiled=True)  10.3 us
    pallas_call x1, Pallas kernels, attention(): call(attention_kernel, (struct((rows, feat), F32), struct((rows, feat), F...  10.1 us
    pallas_call x1, Pallas kernels, run_expert(): call(expert_kernel, pltpu.HBM(arrived.shape, BF16), [WHOLE] * 2 + [IN_HBM...  8.5 us
    ppermute x1, waiting for transfers between devices, on_device(): from_z = lax.ppermute(to_z, 'sec', z_far)  6.33 us
    ppermute x3, waiting for transfers between devices, on_device(): lax.ppermute(part, 'sec', pairs)  4.7 us
    ppermute x3, starting transfers between devices, on_device(): lax.ppermute(part, 'sec', pairs)  4.15 us
  transfers between devices with their start and end apart: 10, of which 5 were waited for; matrix products, arithmetic and copies ran while one was open for 0% of the time, Pallas kernels for 4%

profile of v2, /device:TPU:1, one launch (start us, length us, event | category | flops | bytes accessed | tf_op | source)
XLA Modules:
  0.0 100.1 jit_solution(6746129656817169528)
XLA Ops:
  0.0 10.1 %attention.1 = (f32[256,512]{1,0:T(8,128)S(1)}, f32[256,512]{1,0:T(8,128)S(1)}, bf16[256,1024]{1,0:T(8,128)(2,1)S(1)}) custom-call(s32[2,128]{1,0:T(2,128)} %kept_h.1, s32[2,128]{1,0:T(2,128)} %parent_h.1, f32[1,2048]{1,0:T(1,128)} %bitcast.18, bf16[2,128,2048]{2,1,0:T(8,128)(2,1)} %state_h.1, bf16[2048,512]{1,0:T(8,128)(2,1)} %wq_h.1, ...), custom_call_target="tpu_custom_call" | custom-call | flops 3300000000 | bytes 20000000 | tf_op jit(solution)/shard_map/attention/pallas_call | solution.py:410
  10.1 1.5 %collective-permute-start = (bf16[256,1024]{1,0:T(8,128)(2,1)S(1)}, bf16[256,1024]{1,0:T(8,128)(2,1)S(1)}, u32[]{:S(2)}, u32[]{:S(2)}) collective-permute-start(bf16[256,1024]{1,0:T(8,128)(2,1)S(1)} %get-tuple-element.16), channel_id=1, source_target_pairs={{0,32},{32,0},{64,96},{96,64},{1,33},{33,1},{65,97},{97,65},{2,34}... | collective-permute-start | bytes 1572872 | tf_op jit(solution)/shard_map/head_sum/ppermute | solution.py:577
  11.6 0.0 copy-done.2
  11.6 0.0 copy-done.3
  11.6 1.2 %routing.1 = (bf16[1536,256]{1,0:T(8,128)(2,1)S(1)}, s32[8,256]{1,0:T(8,128)S(1)}) custom-call(s32[2]{0:T(128)S(1)} %copy-done.3, s32[2,2,128]{2,1,0:T(2,128)S(1)} %bitcast.14), custom_call_target="tpu_custom_call" | custom-call | flops 10000000 | bytes 1000000 | tf_op jit(solution)/shard_map/routing/pallas_call | solution.py:454
  12.8 0.1 collective-permute-start.5
  12.9 0.5 collective-permute-start.6
  13.3 0.1 collective-permute-start.7
  13.4 0.0 collective-permute-done.from_core
  13.4 0.1 add_convert_fusion
  13.5 3.8 %collective-permute-start.1 = (bf16[256,512]{1,0:T(8,128)(2,1)S(1)}, bf16[256,512]{1,0:T(8,128)(2,1)S(1)}, u32[]{:S(2)}, u32[]{:S(2)}) collective-permute-start(bf16[256,512]{1,0:T(8,128)(2,1)S(1)} %add_convert_fusion), channel_id=1, source_target_pairs={{0,64},{32,96},{64,0},{96,32},{1,65},{33,97},{65,1},{97,33},{2,66}... | collective-permute-start | bytes 786440 | tf_op jit(solution)/shard_map/head_sum/ppermute | solution.py:579
  17.3 6.3 %collective-permute-done.1.from_z = bf16[256,512]{1,0:T(8,128)(2,1)S(1)} collective-permute-done((bf16[256,512]{1,0:T(8,128)(2,1)S(1)}, bf16[256,512]{1,0:T(8,128)(2,1)S(1)}, u32[]{:S(2)}, u32[]{:S(2)}) %collective-permute-start.1) | collective-permute-done | bytes 262176 | tf_op jit(solution)/shard_map/head_sum/ppermute | solution.py:579
  23.6 0.0 copy-done.1
  23.6 1.6 %dispatch.1 = (f32[256,512]{1,0:T(8,128)S(1)}, bf16[1024,768]{1,0:T(8,128)(2,1)}) custom-call(f32[256,512]{1,0:T(8,128)S(1)} %get-tuple-element.15.keep, bf16[256,1024]{1,0:T(8,128)(2,1)S(1)} %collective-permute-done.from_core, bf16[256,512]{1,0:T(8,128)(2,1)S(1)} %collective-permute-done.1.from_z, f32[1,2048]{1,0:T(1,128)S(1)} %bitcast.11, ...), custom_call_target="tpu_custom_call" | custom-call | flops 300000000 | bytes 4000000 | tf_op jit(solution)/shard_map/dispatch/pallas_call | solution.py:467
  25.2 10.3 %all-to-all-start = ((bf16[128,8,768]{2,1,0:T(8,128)(2,1)}), bf16[128,8,768]{2,1,0:T(8,128)(2,1)S(1)}, u32[]{:S(2)}, u32[]{:S(2)}) async-start(bf16[128,8,768]{2,1,0:T(8,128)(2,1)} %bitcast.17), calls=%async_computation | async-start | bytes 3145728 | tf_op jit(solution)/shard_map/dispatch/all_to_all | solution.py:588
  35.5 0.0 collective-permute-done.5.wg1_h
  35.5 0.0 collective-permute-done.6.wu1_h
  35.5 0.0 collective-permute-done.7.wd1_h
  35.5 24.9 %all-to-all-done = bf16[128,8,768]{2,1,0:T(8,128)(2,1)S(1)} async-done(((bf16[128,8,768]{2,1,0:T(8,128)(2,1)}), bf16[128,8,768]{2,1,0:T(8,128)(2,1)S(1)}, u32[]{:S(2)}, u32[]{:S(2)}) %all-to-all-start) | async-done | bytes 1572896 | tf_op jit(solution)/shard_map/dispatch/all_to_all | solution.py:588
  60.5 8.5 %experts.1 = bf16[1024,768]{1,0:T(8,128)(2,1)} custom-call(bf16[1024,768]{1,0:T(8,128)(2,1)S(1)} %bitcast.9, f32[1,2048]{1,0:T(1,128)S(1)} %bitcast.12, bf16[1,2048,512]{2,1,0:T(8,128)(2,1)} %wg0_h.1, bf16[1,2048,512]{2,1,0:T(8,128)(2,1)} %wu0_h.1, bf16[1,512,2048]{2,1,0:T(8,128)(2,1)} %wd0_h.1, bf16[1,2048,512]{2,1,0:T(8,128)(2,1)} %collective-permute-done.5.wg1_h, ...), custom_call_target="tpu_custom_call" | custom-call | flops 4800000000 | bytes 16000000 | tf_op jit(solution)/shard_map/experts/pallas_call | solution.py:499
  69.0 0.0 copy-start
  69.0 4.0 %all-to-all-start.1 = ((bf16[128,8,768]{2,1,0:T(8,128)(2,1)}), bf16[128,8,768]{2,1,0:T(8,128)(2,1)S(1)}, u32[]{:S(2)}, u32[]{:S(2)}) async-start(bf16[128,8,768]{2,1,0:T(8,128)(2,1)} %bitcast.16), calls=%async_computation.1 | async-start | bytes 3145728 | tf_op jit(solution)/shard_map/experts/all_to_all | solution.py:596
  73.0 0.6 router.1.p0
  73.6 3.7 %collective-permute-start.4 = (f32[8,256]{1,0:T(8,128)S(1)}, f32[8,256]{1,0:T(8,128)S(1)}, u32[]{:S(2)}, u32[]{:S(2)}) collective-permute-start(f32[8,256]{1,0:T(8,128)S(1)} %router.1.p0), channel_id=1, source_target_pairs={{0,96},{32,64},{64,32},{96,0},{1,97},{33,65},{65,33},{97,1},{2,98}... | collective-permute-start | bytes 24584 | tf_op jit(solution)/shard_map/router/ppermute | solution.py:591
  77.3 0.4 collective-permute-start.3
  77.7 0.1 collective-permute-start.2
  77.8 1.4 %collective-permute-done.4.p3 = f32[8,256]{1,0:T(8,128)S(1)} collective-permute-done((f32[8,256]{1,0:T(8,128)S(1)}, f32[8,256]{1,0:T(8,128)S(1)}, u32[]{:S(2)}, u32[]{:S(2)}) %collective-permute-start.4) | collective-permute-done | bytes 8224 | tf_op jit(solution)/shard_map/router/ppermute | solution.py:591
  79.2 3.3 %collective-permute-done.3.p2 = f32[8,256]{1,0:T(8,128)S(1)} collective-permute-done((f32[8,256]{1,0:T(8,128)S(1)}, f32[8,256]{1,0:T(8,128)S(1)}, u32[]{:S(2)}, u32[]{:S(2)}) %collective-permute-start.3) | collective-permute-done | bytes 8224 | tf_op jit(solution)/shard_map/router/ppermute | solution.py:591
  82.5 0.0 collective-permute-done.2.p1
  82.5 0.5 gates.1
  83.0 15.2 %all-to-all-done.1 = bf16[128,8,768]{2,1,0:T(8,128)(2,1)S(1)} async-done(((bf16[128,8,768]{2,1,0:T(8,128)(2,1)}), bf16[128,8,768]{2,1,0:T(8,128)(2,1)S(1)}, u32[]{:S(2)}, u32[]{:S(2)}) %all-to-all-start.1) | async-done | bytes 1572896 | tf_op jit(solution)/shard_map/experts/all_to_all | solution.py:596
  98.1 2.0 %combine.1 = bf16[2,128,512]{2,1,0:T(8,128)(2,1)} custom-call(s32[2]{0:T(128)S(1)} %copy-done.3, f32[256,512]{1,0:T(8,128)S(1)} %get-tuple-element.19.resid, bf16[256,1536]{1,0:T(8,128)(2,1)S(1)} %gates.1, bf16[1024,768]{1,0:T(8,128)(2,1)S(1)} %bitcast.8), custom_call_target="tpu_custom_call" | custom-call | flops 600000000 | bytes 4000000 | tf_op jit(solution)/shard_map/combine/pallas_call | solution.py:525
  (4 shorter events, 0.0 us)
Async XLA Ops:
  0.0 11.6 %copy-start.2 = (s32[2,128,2]{1,2,0:T(2,128)S(1)}, s32[2,128,2]{1,2,0:T(2,128)}, u32[]{:S(2)}) copy-start(s32[2,128,2]{1,2,0:T(2,128)} %param.23) | copy-start | bytes 6148
  0.0 11.6 %copy-start.3 = (s32[2]{0:T(128)S(1)}, s32[2]{0:T(128)}, u32[]{:S(2)}) copy-start(s32[2]{0:T(128)} %alive.3) | copy-start | bytes 28
  0.0 23.6 %copy-start.1 = (f32[2048]{0:T(1024)S(1)}, f32[2048]{0:T(1024)}, u32[]{:S(2)}) copy-start(f32[2048]{0:T(1024)} %param.33) | copy-start | bytes 24580
  10.1 3.4 %collective-permute-start = (bf16[256,1024]{1,0:T(8,128)(2,1)S(1)}, bf16[256,1024]{1,0:T(8,128)(2,1)S(1)}, u32[]{:S(2)}, u32[]{:S(2)}) collective-permute-start(bf16[256,1024]{1,0:T(8,128)(2,1)S(1)} %get-tuple-element.16), channel_id=1, source_target_pairs={{0,32},{32,0},{64,96},{96,64},{1,33},{33,1},{65,97},{97,65},{2,34}... | collective-permute-start | bytes 1572872 | tf_op jit(solution)/shard_map/head_sum/ppermute | solution.py:577
  12.8 22.8 %collective-permute-start.5 = (bf16[1,2048,512]{2,1,0:T(8,128)(2,1)}, bf16[1,2048,512]{2,1,0:T(8,128)(2,1)}, u32[]{:S(2)}, u32[]{:S(2)}) collective-permute-start(bf16[1,2048,512]{2,1,0:T(8,128)(2,1)} %wg0_h.1), channel_id=1, source_target_pairs={{0,32},{32,0},{64,96},{96,64},{1,33},{33,1},{65,97},{97,65},{2,34}... | collective-permute-start | bytes 6291464 | tf_op jit(solution)/shard_map/sibling_weights/ppermute | solution.py:585
  12.9 22.7 %collective-permute-start.6 = (bf16[1,2048,512]{2,1,0:T(8,128)(2,1)}, bf16[1,2048,512]{2,1,0:T(8,128)(2,1)}, u32[]{:S(2)}, u32[]{:S(2)}) collective-permute-start(bf16[1,2048,512]{2,1,0:T(8,128)(2,1)} %wu0_h.1), channel_id=1, source_target_pairs={{0,32},{32,0},{64,96},{96,64},{1,33},{33,1},{65,97},{97,65},{2,34}... | collective-permute-start | bytes 6291464 | tf_op jit(solution)/shard_map/sibling_weights/ppermute | solution.py:585
  13.3 22.2 %collective-permute-start.7 = (bf16[1,512,2048]{2,1,0:T(8,128)(2,1)}, bf16[1,512,2048]{2,1,0:T(8,128)(2,1)}, u32[]{:S(2)}, u32[]{:S(2)}) collective-permute-start(bf16[1,512,2048]{2,1,0:T(8,128)(2,1)} %wd0_h.1), channel_id=1, source_target_pairs={{0,32},{32,0},{64,96},{96,64},{1,33},{33,1},{65,97},{97,65},{2,34}... | collective-permute-start | bytes 6291464 | tf_op jit(solution)/shard_map/sibling_weights/ppermute | solution.py:585
  13.5 10.1 %collective-permute-start.1 = (bf16[256,512]{1,0:T(8,128)(2,1)S(1)}, bf16[256,512]{1,0:T(8,128)(2,1)S(1)}, u32[]{:S(2)}, u32[]{:S(2)}) collective-permute-start(bf16[256,512]{1,0:T(8,128)(2,1)S(1)} %add_convert_fusion), channel_id=1, source_target_pairs={{0,64},{32,96},{64,0},{96,32},{1,65},{33,97},{65,1},{97,33},{2,66}... | collective-permute-start | bytes 786440 | tf_op jit(solution)/shard_map/head_sum/ppermute | solution.py:579
  25.2 35.3 %all-to-all-start = ((bf16[128,8,768]{2,1,0:T(8,128)(2,1)}), bf16[128,8,768]{2,1,0:T(8,128)(2,1)S(1)}, u32[]{:S(2)}, u32[]{:S(2)}) async-start(bf16[128,8,768]{2,1,0:T(8,128)(2,1)} %bitcast.17), calls=%async_computation | async-start | bytes 3145728 | tf_op jit(solution)/shard_map/dispatch/all_to_all | solution.py:588
  69.0 4.0 %copy-start = (bf16[2048,32]{0,1:T(8,128)(2,1)S(1)}, bf16[2048,32]{0,1:T(8,128)(2,1)}, u32[]{:S(2)}) copy-start(bf16[2048,32]{0,1:T(8,128)(2,1)} %param.34) | copy-start | bytes 393220
  69.0 29.1 %all-to-all-start.1 = ((bf16[128,8,768]{2,1,0:T(8,128)(2,1)}), bf16[128,8,768]{2,1,0:T(8,128)(2,1)S(1)}, u32[]{:S(2)}, u32[]{:S(2)}) async-start(bf16[128,8,768]{2,1,0:T(8,128)(2,1)} %bitcast.16), calls=%async_computation.1 | async-start | bytes 3145728 | tf_op jit(solution)/shard_map/experts/all_to_all | solution.py:596
  73.6 5.6 %collective-permute-start.4 = (f32[8,256]{1,0:T(8,128)S(1)}, f32[8,256]{1,0:T(8,128)S(1)}, u32[]{:S(2)}, u32[]{:S(2)}) collective-permute-start(f32[8,256]{1,0:T(8,128)S(1)} %router.1.p0), channel_id=1, source_target_pairs={{0,96},{32,64},{64,32},{96,0},{1,97},{33,65},{65,33},{97,1},{2,98}... | collective-permute-start | bytes 24584 | tf_op jit(solution)/shard_map/router/ppermute | solution.py:591
  77.3 5.2 %collective-permute-start.3 = (f32[8,256]{1,0:T(8,128)S(1)}, f32[8,256]{1,0:T(8,128)S(1)}, u32[]{:S(2)}, u32[]{:S(2)}) collective-permute-start(f32[8,256]{1,0:T(8,128)S(1)} %router.1.p0), channel_id=1, source_target_pairs={{0,64},{32,96},{64,0},{96,32},{1,65},{33,97},{65,1},{97,33},{2,66}... | collective-permute-start | bytes 24584 | tf_op jit(solution)/shard_map/router/ppermute | solution.py:591
  77.7 4.8 %collective-permute-start.2 = (f32[8,256]{1,0:T(8,128)S(1)}, f32[8,256]{1,0:T(8,128)S(1)}, u32[]{:S(2)}, u32[]{:S(2)}) collective-permute-start(f32[8,256]{1,0:T(8,128)S(1)} %router.1.p0), channel_id=1, source_target_pairs={{0,32},{32,0},{64,96},{96,64},{1,33},{33,1},{65,97},{97,65},{2,34}... | collective-permute-start | bytes 24584 | tf_op jit(solution)/shard_map/router/ppermute | solution.py:591

commit v3 on v2

--- a/solution.py
+++ b/solution.py
@@ -15,7 +15,6 @@
 MIB = 1024 * 1024
 WHOLE = pl.BlockSpec(memory_space=pltpu.VMEM)
 IN_HBM = pl.BlockSpec(memory_space=pl.ANY)
-IN_SMEM = pl.BlockSpec(memory_space=pltpu.SMEM)
 
 
 def mm(a, b):
@@ -213,7 +212,7 @@
     users, top, slots = choice.shape
     rows = users * slots
     lane = iota((1, slots), 1)
-    live = jnp.concatenate([lane < alive[u] for u in range(users)], axis=1)
+    live = jnp.concatenate([lane < alive[:, u : u + 1] for u in range(users)], axis=1)
     experts = place.shape[0] // (6 * 8)
     earlier = (iota((rows, rows), 0) < iota((rows, rows), 1)).astype(F32).astype(BF16)
     base = jnp.zeros((experts, 1), F32)
@@ -389,7 +388,7 @@
     tail = slice(feat, arrived.shape[1])
     total = resid[...] + main + jnp.concatenate([bring(1, tail), bring(2, tail)], axis=1)
     for u in range(users):
-        live = iota((slots, feat), 0) < alive[u]
+        live = iota((slots, feat), 0) < alive[:, u : u + 1]
         rows = slice(u * slots, (u + 1) * slots)
         out[u] = jnp.where(live, total[rows], 0.0).astype(BF16)
 
@@ -454,7 +453,7 @@
     return call(
         routing_kernel,
         (struct((6 * 8 * experts, rows), BF16), struct((8, rows), jnp.int32)),
-        [IN_SMEM, WHOLE],
+        [WHOLE] * 2,
         16,
         10_000_000,
         1_000_000,
@@ -525,7 +524,7 @@
     return call(
         combine_kernel,
         struct((users, rows // users, feat), BF16),
-        [IN_SMEM] + [WHOLE] * 3,
+        [WHOLE] * 4,
         24,
         600_000_000,
         4_000_000,
@@ -563,6 +562,7 @@
 
     attention_gain = attention_norm_gain.reshape(1, width)
     expert_gain = expert_norm_gain.reshape(1, width)
+    alive = alive_slot_counts.reshape(1, users)
     choice = jnp.swapaxes(slot_expert_index, 1, 2)
     router = router_projection_weight.T
 
@@ -578,10 +578,10 @@
         to_z = (keep_other + from_core[:, feat:].astype(F32)).astype(BF16)
         from_z = lax.ppermute(to_z, "sec", z_far)
     with jax.named_scope("routing"):
-        place, where = route(alive_slot_counts, choice, experts)
+        place, where = route(alive, choice, experts)
     with jax.named_scope("sibling_weights"):
         weights = [expert_gate_weight, expert_up_weight, expert_down_weight]
-        late = lax.optimization_barrier((*weights, where))[:3]
+        late = lax.optimization_barrier((*weights, to_z))[:3]
         weights = weights + [lax.ppermute(w, "sec", core) for w in late]
     with jax.named_scope("dispatch"):
         resid, message = dispatch(keep_own, from_core, from_z, expert_gain, place)
@@ -595,7 +595,7 @@
         result = run_expert(arrived, expert_gain, weights)
         returned = lax.all_to_all(result, everyone, 0, 0, tiled=True)
     with jax.named_scope("combine"):
-        return combine(alive_slot_counts, resid, gates, returned, users)
+        return combine(alive, resid, gates, returned, users)
 
 
 def solution(mesh):

time: 100 us -> 103 us (1.030)
  blocking collectives: 0 us -> 35.1 us
  waiting for transfers between devices: 51.2 us -> 27.3 us
  starting transfers between devices: 24.4 us -> 14.3 us
  local copies, waits for them, and re-layouts: 0.02 us -> 2.65 us
    all_to_all x0 -> x1, blocking collectives: none -> 35.1 us  [on_device(): arrived = lax.all_to_all(message, everyone, 0, 0, tiled=True)]
    all_to_all x1 -> x0, waiting for transfers between devices: 24.9 us -> none  [on_device(): arrived = lax.all_to_all(message, everyone, 0, 0, tiled=True)]
    all_to_all x1 -> x0, starting transfers between devices: 10.3 us -> none  [on_device(): arrived = lax.all_to_all(message, everyone, 0, 0, tiled=True)]
    unnamed x8 -> x20, local copies, waits for them, and re-layouts: 0.02 us -> 2.65 us
    ppermute x1, waiting for transfers between devices: 0.01 us -> 1.54 us  [on_device(): from_core = lax.ppermute(send, 'sec', core)]
  transfers between devices with their start and end apart: 10 -> 9, of which waited for: 5 -> 5; matrix products, arithmetic and copies ran while one was open for 0% -> 0% of each run, Pallas kernels for 4% -> 3%
where the time goes in v3:
time: 103 us
  blocking collectives  35.1 us (34%)
  waiting for transfers between devices  27.3 us (27%)
  Pallas kernels  23.4 us (23%)
  starting transfers between devices  14.3 us (14%)
  local copies, waits for them, and re-layouts  2.65 us (3%)
    all_to_all x1, blocking collectives, on_device(): arrived = lax.all_to_all(message, everyone, 0, 0, tiled=True)  35.1 us
    all_to_all x1, waiting for transfers between devices, on_device(): returned = lax.all_to_all(result, everyone, 0, 0, tiled=True)  15.2 us
    pallas_call x1, Pallas kernels, attention(): call(attention_kernel, (struct((rows, feat), F32), struct((rows, feat), F...  10.2 us
    pallas_call x1, Pallas kernels, run_expert(): call(expert_kernel, pltpu.HBM(arrived.shape, BF16), [WHOLE] * 2 + [IN_HBM...  8.5 us
    ppermute x1, waiting for transfers between devices, on_device(): from_z = lax.ppermute(to_z, 'sec', z_far)  5.85 us
    ppermute x3, waiting for transfers between devices, on_device(): lax.ppermute(part, 'sec', pairs)  4.71 us
    ppermute x3, starting transfers between devices, on_device(): lax.ppermute(part, 'sec', pairs)  4.15 us
    all_to_all x1, starting transfers between devices, on_device(): returned = lax.all_to_all(result, everyone, 0, 0, tiled=True)  3.99 us
  transfers between devices with their start and end apart: 9, of which 5 were waited for; matrix products, arithmetic and copies ran while one was open for 0% of the time, Pallas kernels for 3%

profile of v3, /device:TPU:1, one launch (start us, length us, event | category | flops | bytes accessed | tf_op | source)
XLA Modules:
  0.0 102.9 jit_solution(7931379451062634443)
XLA Ops:
  0.0 10.2 %attention.1 = (f32[256,512]{1,0:T(8,128)S(1)}, f32[256,512]{1,0:T(8,128)S(1)}, bf16[256,1024]{1,0:T(8,128)(2,1)S(1)}) custom-call(s32[2,128]{1,0:T(2,128)} %kept_h.1, s32[2,128]{1,0:T(2,128)} %parent_h.1, f32[1,2048]{1,0:T(1,128)} %bitcast.21, bf16[2,128,2048]{2,1,0:T(8,128)(2,1)} %state_h.1, bf16[2048,512]{1,0:T(8,128)(2,1)} %wq_h.1, ...), custom_call_target="tpu_custom_call" | custom-call | flops 3300000000 | bytes 20000000 | tf_op jit(solution)/shard_map/attention/pallas_call | solution.py:409
  10.2 1.5 %collective-permute-start = (bf16[256,1024]{1,0:T(8,128)(2,1)S(1)}, bf16[256,1024]{1,0:T(8,128)(2,1)S(1)}, u32[]{:S(2)}, u32[]{:S(2)}) collective-permute-start(bf16[256,1024]{1,0:T(8,128)(2,1)S(1)} %get-tuple-element.16), channel_id=1, source_target_pairs={{0,32},{32,0},{64,96},{96,64},{1,33},{33,1},{65,97},{97,65},{2,34}... | collective-permute-start | bytes 1572872 | tf_op jit(solution)/shard_map/head_sum/ppermute | solution.py:577
  11.7 1.5 %collective-permute-done.from_core = bf16[256,1024]{1,0:T(8,128)(2,1)S(1)} collective-permute-done((bf16[256,1024]{1,0:T(8,128)(2,1)S(1)}, bf16[256,1024]{1,0:T(8,128)(2,1)S(1)}, u32[]{:S(2)}, u32[]{:S(2)}) %collective-permute-start) | collective-permute-done | bytes 524320 | tf_op jit(solution)/shard_map/head_sum/ppermute | solution.py:577
  13.2 0.1 add_convert_fusion
  13.3 0.5 collective-permute-start.5
  13.8 0.1 collective-permute-start.6
  13.9 0.4 collective-permute-start.7
  14.3 3.7 %collective-permute-start.1 = (bf16[256,512]{1,0:T(8,128)(2,1)S(1)}, bf16[256,512]{1,0:T(8,128)(2,1)S(1)}, u32[]{:S(2)}, u32[]{:S(2)}) collective-permute-start(bf16[256,512]{1,0:T(8,128)(2,1)S(1)} %add_convert_fusion), channel_id=1, source_target_pairs={{0,64},{32,96},{64,0},{96,32},{1,65},{33,97},{65,1},{97,33},{2,66}... | collective-permute-start | bytes 786440 | tf_op jit(solution)/shard_map/head_sum/ppermute | solution.py:579
  18.0 0.7 routing.1
  18.7 5.8 %collective-permute-done.1.from_z = bf16[256,512]{1,0:T(8,128)(2,1)S(1)} collective-permute-done((bf16[256,512]{1,0:T(8,128)(2,1)S(1)}, bf16[256,512]{1,0:T(8,128)(2,1)S(1)}, u32[]{:S(2)}, u32[]{:S(2)}) %collective-permute-start.1) | collective-permute-done | bytes 262176 | tf_op jit(solution)/shard_map/head_sum/ppermute | solution.py:579
  24.5 1.6 %dispatch.1 = (f32[256,512]{1,0:T(8,128)S(1)}, bf16[1024,768]{1,0:T(8,128)(2,1)}) custom-call(f32[256,512]{1,0:T(8,128)S(1)} %get-tuple-element.15.keep, bf16[256,1024]{1,0:T(8,128)(2,1)S(1)} %collective-permute-done.from_core, bf16[256,512]{1,0:T(8,128)(2,1)S(1)} %collective-permute-done.1.from_z, f32[1,2048]{1,0:T(1,128)S(1)} %bitcast.12, ...), custom_call_target="tpu_custom_call" | custom-call | flops 300000000 | bytes 4000000 | tf_op jit(solution)/shard_map/dispatch/pallas_call | solution.py:466
  26.1 35.1 %all_to_all.22 = bf16[128,8,768]{2,1,0:T(8,128)(2,1)S(1)} all-to-all(bf16[128,8,768]{2,1,0:T(8,128)(2,1)} %bitcast.20), channel_id=1, replica_groups=mesh['sec'=4,'dp'=32] {'sec','dp'}, dimensions={0} | all-to-all | bytes 3145728 | tf_op jit(solution)/shard_map/dispatch/all_to_all | solution.py:588
  61.2 0.0 collective-permute-done.5.wg1_h
  61.2 0.0 collective-permute-done.6.wu1_h
  61.2 0.0 copy-start.8
  61.2 0.0 collective-permute-done.7.wd1_h
  61.2 1.3 %copy-done.7 = bf16[1,2048,512]{2,1,0:T(8,128)(2,1)} copy-done((bf16[1,2048,512]{2,1,0:T(8,128)(2,1)}, bf16[1,2048,512]{2,1,0:T(8,128)(2,1)S(1)}, u32[]{:S(2)}) %copy-start.7) | copy-done | bytes 2097176
  62.5 0.6 copy-done.8
  63.1 0.7 copy-done.9
  63.8 8.5 %experts.1 = bf16[1024,768]{1,0:T(8,128)(2,1)} custom-call(bf16[1024,768]{1,0:T(8,128)(2,1)S(1)} %bitcast.10, f32[1,2048]{1,0:T(1,128)S(1)} %bitcast.13, bf16[1,2048,512]{2,1,0:T(8,128)(2,1)} %wg0_h.1, bf16[1,2048,512]{2,1,0:T(8,128)(2,1)} %wu0_h.1, bf16[1,512,2048]{2,1,0:T(8,128)(2,1)} %wd0_h.1, bf16[1,2048,512]{2,1,0:T(8,128)(2,1)} %copy-done.7, ...), custom_call_target="tpu_custom_call" | custom-call | flops 4800000000 | bytes 16000000 | tf_op jit(solution)/shard_map/experts/pallas_call | solution.py:498
  72.3 0.0 copy-start
  72.3 4.0 %all-to-all-start.1 = ((bf16[128,8,768]{2,1,0:T(8,128)(2,1)}), bf16[128,8,768]{2,1,0:T(8,128)(2,1)S(1)}, u32[]{:S(2)}, u32[]{:S(2)}) async-start(bf16[128,8,768]{2,1,0:T(8,128)(2,1)} %bitcast.19), calls=%async_computation.1 | async-start | bytes 3145728 | tf_op jit(solution)/shard_map/experts/all_to_all | solution.py:596
  76.4 0.6 router.1.p0
  76.9 3.7 %collective-permute-start.4 = (f32[8,256]{1,0:T(8,128)S(1)}, f32[8,256]{1,0:T(8,128)S(1)}, u32[]{:S(2)}, u32[]{:S(2)}) collective-permute-start(f32[8,256]{1,0:T(8,128)S(1)} %router.1.p0), channel_id=1, source_target_pairs={{0,96},{32,64},{64,32},{96,0},{1,97},{33,65},{65,33},{97,1},{2,98}... | collective-permute-start | bytes 24584 | tf_op jit(solution)/shard_map/router/ppermute | solution.py:591
  80.6 0.4 collective-permute-start.3
  81.0 0.1 collective-permute-start.2
  81.1 1.4 %collective-permute-done.4.p3 = f32[8,256]{1,0:T(8,128)S(1)} collective-permute-done((f32[8,256]{1,0:T(8,128)S(1)}, f32[8,256]{1,0:T(8,128)S(1)}, u32[]{:S(2)}, u32[]{:S(2)}) %collective-permute-start.4) | collective-permute-done | bytes 8224 | tf_op jit(solution)/shard_map/router/ppermute | solution.py:591
  82.5 3.3 %collective-permute-done.3.p2 = f32[8,256]{1,0:T(8,128)S(1)} collective-permute-done((f32[8,256]{1,0:T(8,128)S(1)}, f32[8,256]{1,0:T(8,128)S(1)}, u32[]{:S(2)}, u32[]{:S(2)}) %collective-permute-start.3) | collective-permute-done | bytes 8224 | tf_op jit(solution)/shard_map/router/ppermute | solution.py:591
  85.8 0.0 collective-permute-done.2.p1
  85.8 0.5 gates.1
  86.3 15.2 %all-to-all-done.1 = bf16[128,8,768]{2,1,0:T(8,128)(2,1)S(1)} async-done(((bf16[128,8,768]{2,1,0:T(8,128)(2,1)}), bf16[128,8,768]{2,1,0:T(8,128)(2,1)S(1)}, u32[]{:S(2)}, u32[]{:S(2)}) %all-to-all-start.1) | async-done | bytes 1572896 | tf_op jit(solution)/shard_map/experts/all_to_all | solution.py:596
  101.5 1.4 %combine.1 = bf16[2,128,512]{2,1,0:T(8,128)(2,1)} custom-call(s32[1,2]{1,0:T(1,128)S(1)} %bitcast.18, f32[256,512]{1,0:T(8,128)S(1)} %get-tuple-element.19.resid, bf16[256,1536]{1,0:T(8,128)(2,1)S(1)} %gates.1, bf16[1024,768]{1,0:T(8,128)(2,1)S(1)} %bitcast.9), custom_call_target="tpu_custom_call" | custom-call | flops 600000000 | bytes 4000000 | tf_op jit(solution)/shard_map/combine/pallas_call | solution.py:524
  (15 shorter events, 0.0 us)
Async XLA Ops:
  0.0 13.3 %copy-start.4 = (bf16[1,2048,512]{2,1,0:T(8,128)(2,1)S(1)}, bf16[1,2048,512]{2,1,0:T(8,128)(2,1)}, u32[]{:S(2)}) copy-start(bf16[1,2048,512]{2,1,0:T(8,128)(2,1)} %wg0_h.1) | copy-start | bytes 6291460
  0.0 13.8 %copy-start.5 = (bf16[1,2048,512]{2,1,0:T(8,128)(2,1)S(1)}, bf16[1,2048,512]{2,1,0:T(8,128)(2,1)}, u32[]{:S(2)}) copy-start(bf16[1,2048,512]{2,1,0:T(8,128)(2,1)} %wu0_h.1) | copy-start | bytes 6291460
  0.0 13.9 %copy-start.6 = (bf16[1,512,2048]{2,1,0:T(8,128)(2,1)S(1)}, bf16[1,512,2048]{2,1,0:T(8,128)(2,1)}, u32[]{:S(2)}) copy-start(bf16[1,512,2048]{2,1,0:T(8,128)(2,1)} %wd0_h.1) | copy-start | bytes 6291460
  0.0 17.9 %copy-start.2 = (s32[2,128,2]{1,2,0:T(2,128)S(1)}, s32[2,128,2]{1,2,0:T(2,128)}, u32[]{:S(2)}) copy-start(s32[2,128,2]{1,2,0:T(2,128)} %param.23) | copy-start | bytes 6148
  0.0 17.9 %copy-start.3 = (s32[2]{0:T(128)S(1)}, s32[2]{0:T(128)}, u32[]{:S(2)}) copy-start(s32[2]{0:T(128)} %param.22) | copy-start | bytes 28
  0.0 24.5 %copy-start.1 = (f32[2048]{0:T(1024)S(1)}, f32[2048]{0:T(1024)}, u32[]{:S(2)}) copy-start(f32[2048]{0:T(1024)} %param.33) | copy-start | bytes 24580
  10.2 3.0 %collective-permute-start = (bf16[256,1024]{1,0:T(8,128)(2,1)S(1)}, bf16[256,1024]{1,0:T(8,128)(2,1)S(1)}, u32[]{:S(2)}, u32[]{:S(2)}) collective-permute-start(bf16[256,1024]{1,0:T(8,128)(2,1)S(1)} %get-tuple-element.16), channel_id=1, source_target_pairs={{0,32},{32,0},{64,96},{96,64},{1,33},{33,1},{65,97},{97,65},{2,34}... | collective-permute-start | bytes 1572872 | tf_op jit(solution)/shard_map/head_sum/ppermute | solution.py:577
  13.3 47.9 %collective-permute-start.5 = (bf16[1,2048,512]{2,1,0:T(8,128)(2,1)S(1)}, bf16[1,2048,512]{2,1,0:T(8,128)(2,1)S(1)}, u32[]{:S(2)}, u32[]{:S(2)}) collective-permute-start(bf16[1,2048,512]{2,1,0:T(8,128)(2,1)S(1)} %copy-done.4), channel_id=1, source_target_pairs={{0,32},{32,0},{64,96},{96,64},{1,33},{33,1},{65,97},{97,65},{2,34}... | collective-permute-start | bytes 6291464 | tf_op jit(solution)/shard_map/sibling_weights/ppermute | solution.py:585
  13.8 47.4 %collective-permute-start.6 = (bf16[1,2048,512]{2,1,0:T(8,128)(2,1)S(1)}, bf16[1,2048,512]{2,1,0:T(8,128)(2,1)S(1)}, u32[]{:S(2)}, u32[]{:S(2)}) collective-permute-start(bf16[1,2048,512]{2,1,0:T(8,128)(2,1)S(1)} %copy-done.5), channel_id=1, source_target_pairs={{0,32},{32,0},{64,96},{96,64},{1,33},{33,1},{65,97},{97,65},{2,34}... | collective-permute-start | bytes 6291464 | tf_op jit(solution)/shard_map/sibling_weights/ppermute | solution.py:585
  13.9 47.3 %collective-permute-start.7 = (bf16[1,512,2048]{2,1,0:T(8,128)(2,1)S(1)}, bf16[1,512,2048]{2,1,0:T(8,128)(2,1)S(1)}, u32[]{:S(2)}, u32[]{:S(2)}) collective-permute-start(bf16[1,512,2048]{2,1,0:T(8,128)(2,1)S(1)} %copy-done.6), channel_id=1, source_target_pairs={{0,32},{32,0},{64,96},{96,64},{1,33},{33,1},{65,97},{97,65},{2,34}... | collective-permute-start | bytes 6291464 | tf_op jit(solution)/shard_map/sibling_weights/ppermute | solution.py:585
  14.3 10.2 %collective-permute-start.1 = (bf16[256,512]{1,0:T(8,128)(2,1)S(1)}, bf16[256,512]{1,0:T(8,128)(2,1)S(1)}, u32[]{:S(2)}, u32[]{:S(2)}) collective-permute-start(bf16[256,512]{1,0:T(8,128)(2,1)S(1)} %add_convert_fusion), channel_id=1, source_target_pairs={{0,64},{32,96},{64,0},{96,32},{1,65},{33,97},{65,1},{97,33},{2,66}... | collective-permute-start | bytes 786440 | tf_op jit(solution)/shard_map/head_sum/ppermute | solution.py:579
  61.2 1.3 %copy-start.7 = (bf16[1,2048,512]{2,1,0:T(8,128)(2,1)}, bf16[1,2048,512]{2,1,0:T(8,128)(2,1)S(1)}, u32[]{:S(2)}) copy-start(bf16[1,2048,512]{2,1,0:T(8,128)(2,1)S(1)} %collective-permute-done.5.wg1_h) | copy-start | bytes 6291460
  61.2 1.9 %copy-start.8 = (bf16[1,2048,512]{2,1,0:T(8,128)(2,1)}, bf16[1,2048,512]{2,1,0:T(8,128)(2,1)S(1)}, u32[]{:S(2)}) copy-start(bf16[1,2048,512]{2,1,0:T(8,128)(2,1)S(1)} %collective-permute-done.6.wu1_h) | copy-start | bytes 6291460
  61.2 2.6 %copy-start.9 = (bf16[1,512,2048]{2,1,0:T(8,128)(2,1)}, bf16[1,512,2048]{2,1,0:T(8,128)(2,1)S(1)}, u32[]{:S(2)}) copy-start(bf16[1,512,2048]{2,1,0:T(8,128)(2,1)S(1)} %collective-permute-done.7.wd1_h) | copy-start | bytes 6291460
  72.3 4.0 %copy-start = (bf16[2048,32]{0,1:T(8,128)(2,1)S(1)}, bf16[2048,32]{0,1:T(8,128)(2,1)}, u32[]{:S(2)}) copy-start(bf16[2048,32]{0,1:T(8,128)(2,1)} %param.34) | copy-start | bytes 393220
  72.3 29.1 %all-to-all-start.1 = ((bf16[128,8,768]{2,1,0:T(8,128)(2,1)}), bf16[128,8,768]{2,1,0:T(8,128)(2,1)S(1)}, u32[]{:S(2)}, u32[]{:S(2)}) async-start(bf16[128,8,768]{2,1,0:T(8,128)(2,1)} %bitcast.19), calls=%async_computation.1 | async-start | bytes 3145728 | tf_op jit(solution)/shard_map/experts/all_to_all | solution.py:596
  76.9 5.6 %collective-permute-start.4 = (f32[8,256]{1,0:T(8,128)S(1)}, f32[8,256]{1,0:T(8,128)S(1)}, u32[]{:S(2)}, u32[]{:S(2)}) collective-permute-start(f32[8,256]{1,0:T(8,128)S(1)} %router.1.p0), channel_id=1, source_target_pairs={{0,96},{32,64},{64,32},{96,0},{1,97},{33,65},{65,33},{97,1},{2,98}... | collective-permute-start | bytes 24584 | tf_op jit(solution)/shard_map/router/ppermute | solution.py:591
  80.6 5.2 %collective-permute-start.3 = (f32[8,256]{1,0:T(8,128)S(1)}, f32[8,256]{1,0:T(8,128)S(1)}, u32[]{:S(2)}, u32[]{:S(2)}) collective-permute-start(f32[8,256]{1,0:T(8,128)S(1)} %router.1.p0), channel_id=1, source_target_pairs={{0,64},{32,96},{64,0},{96,32},{1,65},{33,97},{65,1},{97,33},{2,66}... | collective-permute-start | bytes 24584 | tf_op jit(solution)/shard_map/router/ppermute | solution.py:591
  81.0 4.8 %collective-permute-start.2 = (f32[8,256]{1,0:T(8,128)S(1)}, f32[8,256]{1,0:T(8,128)S(1)}, u32[]{:S(2)}, u32[]{:S(2)}) collective-permute-start(f32[8,256]{1,0:T(8,128)S(1)} %router.1.p0), channel_id=1, source_target_pairs={{0,32},{32,0},{64,96},{96,64},{1,33},{33,1},{65,97},{97,65},{2,34}... | collective-permute-start | bytes 24584 | tf_op jit(solution)/shard_map/router/ppermute | solution.py:591

commit v4 on v3

--- a/solution.py
+++ b/solution.py
@@ -80,26 +80,22 @@
     def quarter(n):
         return pl.ds(pl.multiple_of(n * feat, feat), feat)
 
-    order = (sec, 2 * (1 - z) + c, 2 * z + 1 - c, 2 * (1 - z) + 1 - c)
     loads = Loads(sems)
     loads.start("small", (kept_h, kept), (parent_h, parent), (gain_h, gain))
     for u in range(users):
         loads.start_rows(("st", u), state_h.at[u], st.at[u], 2)
-    loads.start_rows("wq", wq_h, wq, 4)
-    loads.start_rows("wk", wk_h, wk, 4)
-    loads.start_rows("wv", wv_h, wv, 4)
+    loads.start_rows("wq", wq_h, wq, 2)
+    loads.start_rows("wk", wk_h, wk, 2)
+    loads.start_rows("wv", wv_h, wv, 2)
     for u in range(users):
         loads.start(
             ("past", u),
-            (dk_h.at[u].reshape(dk.shape[1:]), dk.at[u]),
-            (dv_h.at[u].reshape(dv.shape[1:]), dv.at[u]),
+            (dk_h.at[u], dk.at[u]),
+            (dv_h.at[u], dv.at[u]),
         )
-        loads.start_rows(("kh", u), kh_h.at[u], kh.at[u], 4)
-        loads.start_rows(("vh", u), vh_h.at[u], vh.at[u], 4)
-    loads.start("sq", (state_h.at[:, :, quarter(sec)], sq))
-    loads.start("wo", *[
-        (wo_h.at[:, quarter(n)], wo.at[:, pl.ds(at * feat, feat)]) for at, n in enumerate(order)
-    ])
+        loads.start_rows(("kh", u), kh_h.at[u], kh.at[u], 2)
+        loads.start_rows(("vh", u), vh_h.at[u], vh.at[u], 2)
+    loads.start_rows("wo", wo_h, wo, 2)
 
     loads.wait("small")
     picks = []
@@ -111,14 +107,13 @@
         mean = jnp.mean(xu * xu, axis=-1, keepdims=True)
         nrm[rows, :] = (xu * lax.rsqrt(mean + EPSILON) * gain[...]).astype(BF16)
     loads.wait("wq")
-    q[...] = mm(nrm[...], wq[...]).astype(BF16)
+    q[...] = (mm(nrm[...], wq[...]) * (HD ** (-0.5) * math.log2(math.e))).astype(BF16)
     loads.wait("wk")
     k[...] = mm(nrm[...], wk[...]).astype(BF16)
     loads.wait("wv")
     v[...] = mm(nrm[...], wv[...]).astype(BF16)
 
-    scale = HD ** (-0.5) * math.log2(math.e)
-    steps = dk.shape[1] // slots
+    steps = dk.shape[2]
     chunk = 512
     chunks = [slice(a, a + chunk) for a in range(0, history, chunk)]
     group = 2
@@ -138,10 +133,11 @@
             if h == 0:
                 loads.wait(("past", u))
                 past[u] = []
+                flat = [t[u].reshape(slots * steps, feat) for t in (dk, dv)]
                 for s in range(steps):
                     hot = iota((steps * slots, slots), 0) == parent[u : u + 1, :] * steps + s
                     pick = hot.astype(F32).T.astype(BF16)
-                    past[u].append((mm(pick, dk[u]), mm(pick, dv[u])))
+                    past[u].append(tuple(mm(pick, t) for t in flat))
                 loads.wait(("kh", u))
                 loads.wait(("vh", u))
             qs = q[rows, cols]
@@ -174,7 +170,7 @@
                 for a in range(0, chunk, HD):
                     high = jnp.maximum(high, s[:, a : a + HD])
             if n > 0:
-                e = jnp.exp2((scores[(n - 1) % 2, :, at] - top) * scale)
+                e = jnp.exp2(scores[(n - 1) % 2, :, at] - top)
                 for a in range(0, chunk, HD):
                     mass = mass + e[:, a : a + HD]
                 mixed = mixed + mm(e.astype(BF16), vh[u0, at, cols0])
@@ -190,7 +186,7 @@
             )
             values = [p[:, cols0] for _, p in past[u0]] + [v[rows0, cols0].astype(F32)]
             for s, value in zip(more0, values):
-                e = jnp.exp2((s - top) * scale)
+                e = jnp.exp2(s - top)
                 total = total + e
                 mixed = mixed + e * stack(lambda m: value[:, m])
             mixed = (mixed / total).astype(BF16)
@@ -198,14 +194,13 @@
                 [mixed[m * slots : (m + 1) * slots] for m in range(group)], axis=1
             )
 
-    loads.wait("sq")
     for u in range(users):
-        own[pl.ds(u * slots, slots), :] = mm(picks[u], sq[u]).astype(BF16)
+        own[pl.ds(u * slots, slots), :] = mm(picks[u], st[u, :, quarter(sec)]).astype(BF16)
     loads.wait("wo")
-    out = mm(att[...], wo[...])
-    keep_own[...] = out[:, :feat] + own[...].astype(F32)
-    keep_other[...] = out[:, feat : 2 * feat]
-    send[...] = out[:, 2 * feat :].astype(BF16)
+    keep_own[...] = mm(att[...], wo[:, quarter(sec)]) + own[...].astype(F32)
+    keep_other[...] = mm(att[...], wo[:, quarter(2 * (1 - z) + c)])
+    send[:, :feat] = mm(att[...], wo[:, quarter(2 * z + 1 - c)]).astype(BF16)
+    send[:, feat:] = mm(att[...], wo[:, quarter(2 * (1 - z) + 1 - c)]).astype(BF16)
 
 
 def routing_kernel(alive, choice, place, where):
@@ -425,8 +420,8 @@
             pltpu.VMEM((feat, width), BF16),
             pltpu.VMEM((users, history, feat), BF16),
             pltpu.VMEM((users, history, feat), BF16),
-            pltpu.VMEM((users, slots * steps, feat), BF16),
-            pltpu.VMEM((users, slots * steps, feat), BF16),
+            pltpu.VMEM(past_keys.shape, BF16),
+            pltpu.VMEM(past_keys.shape, BF16),
             pltpu.VMEM((rows, width), BF16),
             pltpu.VMEM((rows, feat), BF16),
             pltpu.VMEM((rows, feat), BF16),
@@ -581,7 +576,7 @@
         place, where = route(alive, choice, experts)
     with jax.named_scope("sibling_weights"):
         weights = [expert_gate_weight, expert_up_weight, expert_down_weight]
-        late = lax.optimization_barrier((*weights, to_z))[:3]
+        late = lax.optimization_barrier((*weights, where))[:3]
         weights = weights + [lax.ppermute(w, "sec", core) for w in late]
     with jax.named_scope("dispatch"):
         resid, message = dispatch(keep_own, from_core, from_z, expert_gain, place)

time: 103 us -> 99.1 us (0.962)
  blocking collectives: 35.1 us -> 0 us
  waiting for transfers between devices: 27.3 us -> 51.4 us
  starting transfers between devices: 14.3 us -> 24.3 us
  local copies, waits for them, and re-layouts: 2.65 us -> 0.02 us
    all_to_all x1 -> x0, blocking collectives: 35.1 us -> none  [on_device(): arrived = lax.all_to_all(message, everyone, 0, 0, tiled=True)]
    all_to_all x0 -> x1, waiting for transfers between devices: none -> 24.9 us  [on_device(): arrived = lax.all_to_all(message, everyone, 0, 0, tiled=True)]
    all_to_all x0 -> x1, starting transfers between devices: none -> 10.3 us  [on_device(): arrived = lax.all_to_all(message, everyone, 0, 0, tiled=True)]
    unnamed x20 -> x8, local copies, waits for them, and re-layouts: 2.65 us -> 0.02 us
    ppermute x1, waiting for transfers between devices: 1.54 us -> 0.15 us  [on_device(): from_core = lax.ppermute(send, 'sec', core)]
  transfers between devices with their start and end apart: 9 -> 10, of which waited for: 5 -> 6; matrix products, arithmetic and copies ran while one was open for 0% -> 0% of each run, Pallas kernels for 3% -> 3%
where the time goes in v4:
time: 99.1 us; the launch traced here: 98.8 us
  waiting for transfers between devices  51.4 us (52%)
  starting transfers between devices  24.3 us (25%)
  Pallas kernels  22.9 us (23%)
    all_to_all x1, waiting for transfers between devices, on_device(): arrived = lax.all_to_all(message, everyone, 0, 0, tiled=True)  24.9 us
    all_to_all x1, waiting for transfers between devices, on_device(): returned = lax.all_to_all(result, everyone, 0, 0, tiled=True)  15.2 us
    all_to_all x1, starting transfers between devices, on_device(): arrived = lax.all_to_all(message, everyone, 0, 0, tiled=True)  10.3 us
    pallas_call x1, Pallas kernels, attention(): call(attention_kernel, (struct((rows, feat), F32), struct((rows, feat), F...  9.63 us
    pallas_call x1, Pallas kernels, run_expert(): call(expert_kernel, pltpu.HBM(arrived.shape, BF16), [WHOLE] * 2 + [IN_HBM...  8.5 us
    ppermute x1, waiting for transfers between devices, on_device(): from_z = lax.ppermute(to_z, 'sec', z_far)  6.38 us
    ppermute x3, waiting for transfers between devices, on_device(): lax.ppermute(part, 'sec', pairs)  4.7 us
    ppermute x3, starting transfers between devices, on_device(): lax.ppermute(part, 'sec', pairs)  4.15 us
  transfers between devices with their start and end apart: 10, of which 6 were waited for; matrix products, arithmetic and copies ran while one was open for 0% of the time, Pallas kernels for 3%

profile of v4, /device:TPU:1, one launch (start us, length us, event | category | flops | bytes accessed | tf_op | source)
XLA Modules:
  0.0 98.8 jit_solution(16689479326113779411)
XLA Ops:
  0.0 9.6 %attention.1 = (f32[256,512]{1,0:T(8,128)S(1)}, f32[256,512]{1,0:T(8,128)S(1)}, bf16[256,1024]{1,0:T(8,128)(2,1)S(1)}) custom-call(s32[2,128]{1,0:T(2,128)} %kept_h.1, s32[2,128]{1,0:T(2,128)} %parent_h.1, f32[1,2048]{1,0:T(1,128)} %bitcast.21, bf16[2,128,2048]{2,1,0:T(8,128)(2,1)} %state_h.1, bf16[2048,512]{1,0:T(8,128)(2,1)} %wq_h.1, ...), custom_call_target="tpu_custom_call" | custom-call | flops 3300000000 | bytes 20000000 | tf_op jit(solution)/shard_map/attention/pallas_call | solution.py:404
  9.6 1.5 %collective-permute-start = (bf16[256,1024]{1,0:T(8,128)(2,1)S(1)}, bf16[256,1024]{1,0:T(8,128)(2,1)S(1)}, u32[]{:S(2)}, u32[]{:S(2)}) collective-permute-start(bf16[256,1024]{1,0:T(8,128)(2,1)S(1)} %get-tuple-element.16), channel_id=1, source_target_pairs={{0,32},{32,0},{64,96},{96,64},{1,33},{33,1},{65,97},{97,65},{2,34}... | collective-permute-start | bytes 1572872 | tf_op jit(solution)/shard_map/head_sum/ppermute | solution.py:572
  11.1 0.0 copy-done.2
  11.1 0.0 copy-done.3
  11.1 0.7 routing.1
  11.8 0.1 collective-permute-start.5
  12.0 0.5 collective-permute-start.6
  12.4 0.1 collective-permute-start.7
  12.5 0.2 collective-permute-done.from_core
  12.7 0.1 add_convert_fusion
  12.7 3.8 %collective-permute-start.1 = (bf16[256,512]{1,0:T(8,128)(2,1)S(1)}, bf16[256,512]{1,0:T(8,128)(2,1)S(1)}, u32[]{:S(2)}, u32[]{:S(2)}) collective-permute-start(bf16[256,512]{1,0:T(8,128)(2,1)S(1)} %add_convert_fusion), channel_id=1, source_target_pairs={{0,64},{32,96},{64,0},{96,32},{1,65},{33,97},{65,1},{97,33},{2,66}... | collective-permute-start | bytes 786440 | tf_op jit(solution)/shard_map/head_sum/ppermute | solution.py:574
  16.5 6.4 %collective-permute-done.1.from_z = bf16[256,512]{1,0:T(8,128)(2,1)S(1)} collective-permute-done((bf16[256,512]{1,0:T(8,128)(2,1)S(1)}, bf16[256,512]{1,0:T(8,128)(2,1)S(1)}, u32[]{:S(2)}, u32[]{:S(2)}) %collective-permute-start.1) | collective-permute-done | bytes 262176 | tf_op jit(solution)/shard_map/head_sum/ppermute | solution.py:574
  22.9 0.0 copy-done.1
  22.9 1.6 %dispatch.1 = (f32[256,512]{1,0:T(8,128)S(1)}, bf16[1024,768]{1,0:T(8,128)(2,1)}) custom-call(f32[256,512]{1,0:T(8,128)S(1)} %get-tuple-element.15.keep, bf16[256,1024]{1,0:T(8,128)(2,1)S(1)} %collective-permute-done.from_core, bf16[256,512]{1,0:T(8,128)(2,1)S(1)} %collective-permute-done.1.from_z, f32[1,2048]{1,0:T(1,128)S(1)} %bitcast.12, ...), custom_call_target="tpu_custom_call" | custom-call | flops 300000000 | bytes 4000000 | tf_op jit(solution)/shard_map/dispatch/pallas_call | solution.py:461
  24.5 10.3 %all-to-all-start = ((bf16[128,8,768]{2,1,0:T(8,128)(2,1)}), bf16[128,8,768]{2,1,0:T(8,128)(2,1)S(1)}, u32[]{:S(2)}, u32[]{:S(2)}) async-start(bf16[128,8,768]{2,1,0:T(8,128)(2,1)} %bitcast.20), calls=%async_computation | async-start | bytes 3145728 | tf_op jit(solution)/shard_map/dispatch/all_to_all | solution.py:583
  34.7 0.0 collective-permute-done.5.wg1_h
  34.7 0.0 collective-permute-done.6.wu1_h
  34.8 0.0 collective-permute-done.7.wd1_h
  34.8 24.9 %all-to-all-done = bf16[128,8,768]{2,1,0:T(8,128)(2,1)S(1)} async-done(((bf16[128,8,768]{2,1,0:T(8,128)(2,1)}), bf16[128,8,768]{2,1,0:T(8,128)(2,1)S(1)}, u32[]{:S(2)}, u32[]{:S(2)}) %all-to-all-start) | async-done | bytes 1572896 | tf_op jit(solution)/shard_map/dispatch/all_to_all | solution.py:583
  59.7 8.5 %experts.1 = bf16[1024,768]{1,0:T(8,128)(2,1)} custom-call(bf16[1024,768]{1,0:T(8,128)(2,1)S(1)} %bitcast.10, f32[1,2048]{1,0:T(1,128)S(1)} %bitcast.13, bf16[1,2048,512]{2,1,0:T(8,128)(2,1)} %wg0_h.1, bf16[1,2048,512]{2,1,0:T(8,128)(2,1)} %wu0_h.1, bf16[1,512,2048]{2,1,0:T(8,128)(2,1)} %wd0_h.1, bf16[1,2048,512]{2,1,0:T(8,128)(2,1)} %collective-permute-done.5.wg1_h, ...), custom_call_target="tpu_custom_call" | custom-call | flops 4800000000 | bytes 16000000 | tf_op jit(solution)/shard_map/experts/pallas_call | solution.py:493
  68.2 0.0 copy-start
  68.2 4.0 %all-to-all-start.1 = ((bf16[128,8,768]{2,1,0:T(8,128)(2,1)}), bf16[128,8,768]{2,1,0:T(8,128)(2,1)S(1)}, u32[]{:S(2)}, u32[]{:S(2)}) async-start(bf16[128,8,768]{2,1,0:T(8,128)(2,1)} %bitcast.19), calls=%async_computation.1 | async-start | bytes 3145728 | tf_op jit(solution)/shard_map/experts/all_to_all | solution.py:591
  72.2 0.6 router.1.p0
  72.8 3.7 %collective-permute-start.4 = (f32[8,256]{1,0:T(8,128)S(1)}, f32[8,256]{1,0:T(8,128)S(1)}, u32[]{:S(2)}, u32[]{:S(2)}) collective-permute-start(f32[8,256]{1,0:T(8,128)S(1)} %router.1.p0), channel_id=1, source_target_pairs={{0,96},{32,64},{64,32},{96,0},{1,97},{33,65},{65,33},{97,1},{2,98}... | collective-permute-start | bytes 24584 | tf_op jit(solution)/shard_map/router/ppermute | solution.py:586
  76.5 0.4 collective-permute-start.3
  76.9 0.1 collective-permute-start.2
  77.0 1.4 %collective-permute-done.4.p3 = f32[8,256]{1,0:T(8,128)S(1)} collective-permute-done((f32[8,256]{1,0:T(8,128)S(1)}, f32[8,256]{1,0:T(8,128)S(1)}, u32[]{:S(2)}, u32[]{:S(2)}) %collective-permute-start.4) | collective-permute-done | bytes 8224 | tf_op jit(solution)/shard_map/router/ppermute | solution.py:586
  78.4 3.3 %collective-permute-done.3.p2 = f32[8,256]{1,0:T(8,128)S(1)} collective-permute-done((f32[8,256]{1,0:T(8,128)S(1)}, f32[8,256]{1,0:T(8,128)S(1)}, u32[]{:S(2)}, u32[]{:S(2)}) %collective-permute-start.3) | collective-permute-done | bytes 8224 | tf_op jit(solution)/shard_map/router/ppermute | solution.py:586
  81.7 0.0 collective-permute-done.2.p1
  81.7 0.5 gates.1
  82.2 15.2 %all-to-all-done.1 = bf16[128,8,768]{2,1,0:T(8,128)(2,1)S(1)} async-done(((bf16[128,8,768]{2,1,0:T(8,128)(2,1)}), bf16[128,8,768]{2,1,0:T(8,128)(2,1)S(1)}, u32[]{:S(2)}, u32[]{:S(2)}) %all-to-all-start.1) | async-done | bytes 1572896 | tf_op jit(solution)/shard_map/experts/all_to_all | solution.py:591
  97.4 1.4 %combine.1 = bf16[2,128,512]{2,1,0:T(8,128)(2,1)} custom-call(s32[1,2]{1,0:T(1,128)S(1)} %bitcast.18, f32[256,512]{1,0:T(8,128)S(1)} %get-tuple-element.19.resid, bf16[256,1536]{1,0:T(8,128)(2,1)S(1)} %gates.1, bf16[1024,768]{1,0:T(8,128)(2,1)S(1)} %bitcast.9), custom_call_target="tpu_custom_call" | custom-call | flops 600000000 | bytes 4000000 | tf_op jit(solution)/shard_map/combine/pallas_call | solution.py:519
  (4 shorter events, 0.0 us)
Async XLA Ops:
  0.0 11.1 %copy-start.2 = (s32[2,128,2]{1,2,0:T(2,128)S(1)}, s32[2,128,2]{1,2,0:T(2,128)}, u32[]{:S(2)}) copy-start(s32[2,128,2]{1,2,0:T(2,128)} %param.23) | copy-start | bytes 6148
  0.0 11.1 %copy-start.3 = (s32[2]{0:T(128)S(1)}, s32[2]{0:T(128)}, u32[]{:S(2)}) copy-start(s32[2]{0:T(128)} %param.22) | copy-start | bytes 28
  0.0 22.9 %copy-start.1 = (f32[2048]{0:T(1024)S(1)}, f32[2048]{0:T(1024)}, u32[]{:S(2)}) copy-start(f32[2048]{0:T(1024)} %param.33) | copy-start | bytes 24580
  9.6 3.0 %collective-permute-start = (bf16[256,1024]{1,0:T(8,128)(2,1)S(1)}, bf16[256,1024]{1,0:T(8,128)(2,1)S(1)}, u32[]{:S(2)}, u32[]{:S(2)}) collective-permute-start(bf16[256,1024]{1,0:T(8,128)(2,1)S(1)} %get-tuple-element.16), channel_id=1, source_target_pairs={{0,32},{32,0},{64,96},{96,64},{1,33},{33,1},{65,97},{97,65},{2,34}... | collective-permute-start | bytes 1572872 | tf_op jit(solution)/shard_map/head_sum/ppermute | solution.py:572
  11.8 22.9 %collective-permute-start.5 = (bf16[1,2048,512]{2,1,0:T(8,128)(2,1)}, bf16[1,2048,512]{2,1,0:T(8,128)(2,1)}, u32[]{:S(2)}, u32[]{:S(2)}) collective-permute-start(bf16[1,2048,512]{2,1,0:T(8,128)(2,1)} %wg0_h.1), channel_id=1, source_target_pairs={{0,32},{32,0},{64,96},{96,64},{1,33},{33,1},{65,97},{97,65},{2,34}... | collective-permute-start | bytes 6291464 | tf_op jit(solution)/shard_map/sibling_weights/ppermute | solution.py:580
  12.0 22.8 %collective-permute-start.6 = (bf16[1,2048,512]{2,1,0:T(8,128)(2,1)}, bf16[1,2048,512]{2,1,0:T(8,128)(2,1)}, u32[]{:S(2)}, u32[]{:S(2)}) collective-permute-start(bf16[1,2048,512]{2,1,0:T(8,128)(2,1)} %wu0_h.1), channel_id=1, source_target_pairs={{0,32},{32,0},{64,96},{96,64},{1,33},{33,1},{65,97},{97,65},{2,34}... | collective-permute-start | bytes 6291464 | tf_op jit(solution)/shard_map/sibling_weights/ppermute | solution.py:580
  12.4 22.3 %collective-permute-start.7 = (bf16[1,512,2048]{2,1,0:T(8,128)(2,1)}, bf16[1,512,2048]{2,1,0:T(8,128)(2,1)}, u32[]{:S(2)}, u32[]{:S(2)}) collective-permute-start(bf16[1,512,2048]{2,1,0:T(8,128)(2,1)} %wd0_h.1), channel_id=1, source_target_pairs={{0,32},{32,0},{64,96},{96,64},{1,33},{33,1},{65,97},{97,65},{2,34}... | collective-permute-start | bytes 6291464 | tf_op jit(solution)/shard_map/sibling_weights/ppermute | solution.py:580
  12.7 10.1 %collective-permute-start.1 = (bf16[256,512]{1,0:T(8,128)(2,1)S(1)}, bf16[256,512]{1,0:T(8,128)(2,1)S(1)}, u32[]{:S(2)}, u32[]{:S(2)}) collective-permute-start(bf16[256,512]{1,0:T(8,128)(2,1)S(1)} %add_convert_fusion), channel_id=1, source_target_pairs={{0,64},{32,96},{64,0},{96,32},{1,65},{33,97},{65,1},{97,33},{2,66}... | collective-permute-start | bytes 786440 | tf_op jit(solution)/shard_map/head_sum/ppermute | solution.py:574
  24.5 35.2 %all-to-all-start = ((bf16[128,8,768]{2,1,0:T(8,128)(2,1)}), bf16[128,8,768]{2,1,0:T(8,128)(2,1)S(1)}, u32[]{:S(2)}, u32[]{:S(2)}) async-start(bf16[128,8,768]{2,1,0:T(8,128)(2,1)} %bitcast.20), calls=%async_computation | async-start | bytes 3145728 | tf_op jit(solution)/shard_map/dispatch/all_to_all | solution.py:583
  68.2 4.0 %copy-start = (bf16[2048,32]{0,1:T(8,128)(2,1)S(1)}, bf16[2048,32]{0,1:T(8,128)(2,1)}, u32[]{:S(2)}) copy-start(bf16[2048,32]{0,1:T(8,128)(2,1)} %param.34) | copy-start | bytes 393220
  68.2 29.1 %all-to-all-start.1 = ((bf16[128,8,768]{2,1,0:T(8,128)(2,1)}), bf16[128,8,768]{2,1,0:T(8,128)(2,1)S(1)}, u32[]{:S(2)}, u32[]{:S(2)}) async-start(bf16[128,8,768]{2,1,0:T(8,128)(2,1)} %bitcast.19), calls=%async_computation.1 | async-start | bytes 3145728 | tf_op jit(solution)/shard_map/experts/all_to_all | solution.py:591
  72.8 5.6 %collective-permute-start.4 = (f32[8,256]{1,0:T(8,128)S(1)}, f32[8,256]{1,0:T(8,128)S(1)}, u32[]{:S(2)}, u32[]{:S(2)}) collective-permute-start(f32[8,256]{1,0:T(8,128)S(1)} %router.1.p0), channel_id=1, source_target_pairs={{0,96},{32,64},{64,32},{96,0},{1,97},{33,65},{65,33},{97,1},{2,98}... | collective-permute-start | bytes 24584 | tf_op jit(solution)/shard_map/router/ppermute | solution.py:586
  76.5 5.2 %collective-permute-start.3 = (f32[8,256]{1,0:T(8,128)S(1)}, f32[8,256]{1,0:T(8,128)S(1)}, u32[]{:S(2)}, u32[]{:S(2)}) collective-permute-start(f32[8,256]{1,0:T(8,128)S(1)} %router.1.p0), channel_id=1, source_target_pairs={{0,64},{32,96},{64,0},{96,32},{1,65},{33,97},{65,1},{97,33},{2,66}... | collective-permute-start | bytes 24584 | tf_op jit(solution)/shard_map/router/ppermute | solution.py:586
  76.9 4.8 %collective-permute-start.2 = (f32[8,256]{1,0:T(8,128)S(1)}, f32[8,256]{1,0:T(8,128)S(1)}, u32[]{:S(2)}, u32[]{:S(2)}) collective-permute-start(f32[8,256]{1,0:T(8,128)S(1)} %router.1.p0), channel_id=1, source_target_pairs={{0,32},{32,0},{64,96},{96,64},{1,33},{33,1},{65,97},{97,65},{2,34}... | collective-permute-start | bytes 24584 | tf_op jit(solution)/shard_map/router/ppermute | solution.py:586

commit v5 on v4

--- a/solution.py
+++ b/solution.py
@@ -347,8 +347,16 @@
     plain = x[...].astype(F32) * (1.0 / gain[...])
     scale = lax.rsqrt(jnp.mean(plain * plain, axis=-1, keepdims=True) + EPSILON)
     for n, (wg, wu) in enumerate(((wg0, wu0), (wg1, wu1))):
-        loads.wait(2 * n)
-        g = mm(x[...], wg[...]) * scale
+        if n == 0:
+            for copy in loads.copies[0][:2]:
+                copy.wait()
+            g = mm(x[:, : width // 2], wg[: width // 2, :])
+            for copy in loads.copies[0][2:]:
+                copy.wait()
+            g = (g + mm(x[:, width // 2 :], wg[width // 2 :, :])) * scale
+        else:
+            loads.wait(2 * n)
+            g = mm(x[...], wg[...]) * scale
         loads.wait(2 * n + 1)
         u = mm(x[...], wu[...]) * scale
         act[:, n * hidden : (n + 1) * hidden] = (g / (1.0 + jnp.exp(-g)) * u).astype(BF16)

time: 99.1 us -> 99 us (level)
  no operation moved by 1% of the time
where the time goes in v5:
time: 99 us; the launch traced here: 98.8 us
  waiting for transfers between devices  51.4 us (52%)
  starting transfers between devices  24.3 us (25%)
  Pallas kernels  22.9 us (23%)
    all_to_all x1, waiting for transfers between devices, on_device(): arrived = lax.all_to_all(message, everyone, 0, 0, tiled=True)  24.9 us
    all_to_all x1, waiting for transfers between devices, on_device(): returned = lax.all_to_all(result, everyone, 0, 0, tiled=True)  15.2 us
    all_to_all x1, starting transfers between devices, on_device(): arrived = lax.all_to_all(message, everyone, 0, 0, tiled=True)  10.3 us
    pallas_call x1, Pallas kernels, attention(): call(attention_kernel, (struct((rows, feat), F32), struct((rows, feat), F...  9.63 us
    pallas_call x1, Pallas kernels, run_expert(): call(expert_kernel, pltpu.HBM(arrived.shape, BF16), [WHOLE] * 2 + [IN_HBM...  8.48 us
    ppermute x1, waiting for transfers between devices, on_device(): from_z = lax.ppermute(to_z, 'sec', z_far)  6.38 us
    ppermute x3, waiting for transfers between devices, on_device(): lax.ppermute(part, 'sec', pairs)  4.7 us
    ppermute x3, starting transfers between devices, on_device(): lax.ppermute(part, 'sec', pairs)  4.15 us
  transfers between devices with their start and end apart: 10, of which 6 were waited for; matrix products, arithmetic and copies ran while one was open for 0% of the time, Pallas kernels for 3%

profile of v5, /device:TPU:1, one launch (start us, length us, event | category | flops | bytes accessed | tf_op | source)
XLA Modules:
  0.0 98.8 jit_solution(13897992212770302709)
XLA Ops:
  0.0 9.6 %attention.1 = (f32[256,512]{1,0:T(8,128)S(1)}, f32[256,512]{1,0:T(8,128)S(1)}, bf16[256,1024]{1,0:T(8,128)(2,1)S(1)}) custom-call(s32[2,128]{1,0:T(2,128)} %kept_h.1, s32[2,128]{1,0:T(2,128)} %parent_h.1, f32[1,2048]{1,0:T(1,128)} %bitcast.21, bf16[2,128,2048]{2,1,0:T(8,128)(2,1)} %state_h.1, bf16[2048,512]{1,0:T(8,128)(2,1)} %wq_h.1, ...), custom_call_target="tpu_custom_call" | custom-call | flops 3300000000 | bytes 20000000 | tf_op jit(solution)/shard_map/attention/pallas_call | solution.py:412
  9.6 1.5 %collective-permute-start = (bf16[256,1024]{1,0:T(8,128)(2,1)S(1)}, bf16[256,1024]{1,0:T(8,128)(2,1)S(1)}, u32[]{:S(2)}, u32[]{:S(2)}) collective-permute-start(bf16[256,1024]{1,0:T(8,128)(2,1)S(1)} %get-tuple-element.16), channel_id=1, source_target_pairs={{0,32},{32,0},{64,96},{96,64},{1,33},{33,1},{65,97},{97,65},{2,34}... | collective-permute-start | bytes 1572872 | tf_op jit(solution)/shard_map/head_sum/ppermute | solution.py:580
  11.1 0.0 copy-done.2
  11.1 0.0 copy-done.3
  11.1 0.7 routing.1
  11.8 0.1 collective-permute-start.5
  12.0 0.5 collective-permute-start.6
  12.4 0.1 collective-permute-start.7
  12.5 0.2 collective-permute-done.from_core
  12.7 0.1 add_convert_fusion
  12.7 3.8 %collective-permute-start.1 = (bf16[256,512]{1,0:T(8,128)(2,1)S(1)}, bf16[256,512]{1,0:T(8,128)(2,1)S(1)}, u32[]{:S(2)}, u32[]{:S(2)}) collective-permute-start(bf16[256,512]{1,0:T(8,128)(2,1)S(1)} %add_convert_fusion), channel_id=1, source_target_pairs={{0,64},{32,96},{64,0},{96,32},{1,65},{33,97},{65,1},{97,33},{2,66}... | collective-permute-start | bytes 786440 | tf_op jit(solution)/shard_map/head_sum/ppermute | solution.py:582
  16.5 6.4 %collective-permute-done.1.from_z = bf16[256,512]{1,0:T(8,128)(2,1)S(1)} collective-permute-done((bf16[256,512]{1,0:T(8,128)(2,1)S(1)}, bf16[256,512]{1,0:T(8,128)(2,1)S(1)}, u32[]{:S(2)}, u32[]{:S(2)}) %collective-permute-start.1) | collective-permute-done | bytes 262176 | tf_op jit(solution)/shard_map/head_sum/ppermute | solution.py:582
  22.9 0.0 copy-done.1
  22.9 1.6 %dispatch.1 = (f32[256,512]{1,0:T(8,128)S(1)}, bf16[1024,768]{1,0:T(8,128)(2,1)}) custom-call(f32[256,512]{1,0:T(8,128)S(1)} %get-tuple-element.15.keep, bf16[256,1024]{1,0:T(8,128)(2,1)S(1)} %collective-permute-done.from_core, bf16[256,512]{1,0:T(8,128)(2,1)S(1)} %collective-permute-done.1.from_z, f32[1,2048]{1,0:T(1,128)S(1)} %bitcast.12, ...), custom_call_target="tpu_custom_call" | custom-call | flops 300000000 | bytes 4000000 | tf_op jit(solution)/shard_map/dispatch/pallas_call | solution.py:469
  24.5 10.3 %all-to-all-start = ((bf16[128,8,768]{2,1,0:T(8,128)(2,1)}), bf16[128,8,768]{2,1,0:T(8,128)(2,1)S(1)}, u32[]{:S(2)}, u32[]{:S(2)}) async-start(bf16[128,8,768]{2,1,0:T(8,128)(2,1)} %bitcast.20), calls=%async_computation | async-start | bytes 3145728 | tf_op jit(solution)/shard_map/dispatch/all_to_all | solution.py:591
  34.7 0.0 collective-permute-done.5.wg1_h
  34.7 0.0 collective-permute-done.6.wu1_h
  34.8 0.0 collective-permute-done.7.wd1_h
  34.8 24.9 %all-to-all-done = bf16[128,8,768]{2,1,0:T(8,128)(2,1)S(1)} async-done(((bf16[128,8,768]{2,1,0:T(8,128)(2,1)}), bf16[128,8,768]{2,1,0:T(8,128)(2,1)S(1)}, u32[]{:S(2)}, u32[]{:S(2)}) %all-to-all-start) | async-done | bytes 1572896 | tf_op jit(solution)/shard_map/dispatch/all_to_all | solution.py:591
  59.7 8.5 %experts.1 = bf16[1024,768]{1,0:T(8,128)(2,1)} custom-call(bf16[1024,768]{1,0:T(8,128)(2,1)S(1)} %bitcast.10, f32[1,2048]{1,0:T(1,128)S(1)} %bitcast.13, bf16[1,2048,512]{2,1,0:T(8,128)(2,1)} %wg0_h.1, bf16[1,2048,512]{2,1,0:T(8,128)(2,1)} %wu0_h.1, bf16[1,512,2048]{2,1,0:T(8,128)(2,1)} %wd0_h.1, bf16[1,2048,512]{2,1,0:T(8,128)(2,1)} %collective-permute-done.5.wg1_h, ...), custom_call_target="tpu_custom_call" | custom-call | flops 4800000000 | bytes 16000000 | tf_op jit(solution)/shard_map/experts/pallas_call | solution.py:501
  68.2 0.0 copy-start
  68.2 4.0 %all-to-all-start.1 = ((bf16[128,8,768]{2,1,0:T(8,128)(2,1)}), bf16[128,8,768]{2,1,0:T(8,128)(2,1)S(1)}, u32[]{:S(2)}, u32[]{:S(2)}) async-start(bf16[128,8,768]{2,1,0:T(8,128)(2,1)} %bitcast.19), calls=%async_computation.1 | async-start | bytes 3145728 | tf_op jit(solution)/shard_map/experts/all_to_all | solution.py:599
  72.2 0.6 router.1.p0
  72.8 3.7 %collective-permute-start.4 = (f32[8,256]{1,0:T(8,128)S(1)}, f32[8,256]{1,0:T(8,128)S(1)}, u32[]{:S(2)}, u32[]{:S(2)}) collective-permute-start(f32[8,256]{1,0:T(8,128)S(1)} %router.1.p0), channel_id=1, source_target_pairs={{0,96},{32,64},{64,32},{96,0},{1,97},{33,65},{65,33},{97,1},{2,98}... | collective-permute-start | bytes 24584 | tf_op jit(solution)/shard_map/router/ppermute | solution.py:594
  76.5 0.4 collective-permute-start.3
  76.9 0.1 collective-permute-start.2
  77.0 1.4 %collective-permute-done.4.p3 = f32[8,256]{1,0:T(8,128)S(1)} collective-permute-done((f32[8,256]{1,0:T(8,128)S(1)}, f32[8,256]{1,0:T(8,128)S(1)}, u32[]{:S(2)}, u32[]{:S(2)}) %collective-permute-start.4) | collective-permute-done | bytes 8224 | tf_op jit(solution)/shard_map/router/ppermute | solution.py:594
  78.4 3.3 %collective-permute-done.3.p2 = f32[8,256]{1,0:T(8,128)S(1)} collective-permute-done((f32[8,256]{1,0:T(8,128)S(1)}, f32[8,256]{1,0:T(8,128)S(1)}, u32[]{:S(2)}, u32[]{:S(2)}) %collective-permute-start.3) | collective-permute-done | bytes 8224 | tf_op jit(solution)/shard_map/router/ppermute | solution.py:594
  81.7 0.0 collective-permute-done.2.p1
  81.7 0.5 gates.1
  82.2 15.2 %all-to-all-done.1 = bf16[128,8,768]{2,1,0:T(8,128)(2,1)S(1)} async-done(((bf16[128,8,768]{2,1,0:T(8,128)(2,1)}), bf16[128,8,768]{2,1,0:T(8,128)(2,1)S(1)}, u32[]{:S(2)}, u32[]{:S(2)}) %all-to-all-start.1) | async-done | bytes 1572896 | tf_op jit(solution)/shard_map/experts/all_to_all | solution.py:599
  97.3 1.4 %combine.1 = bf16[2,128,512]{2,1,0:T(8,128)(2,1)} custom-call(s32[1,2]{1,0:T(1,128)S(1)} %bitcast.18, f32[256,512]{1,0:T(8,128)S(1)} %get-tuple-element.19.resid, bf16[256,1536]{1,0:T(8,128)(2,1)S(1)} %gates.1, bf16[1024,768]{1,0:T(8,128)(2,1)S(1)} %bitcast.9), custom_call_target="tpu_custom_call" | custom-call | flops 600000000 | bytes 4000000 | tf_op jit(solution)/shard_map/combine/pallas_call | solution.py:527
  (4 shorter events, 0.0 us)
Async XLA Ops:
  0.0 11.1 %copy-start.2 = (s32[2,128,2]{1,2,0:T(2,128)S(1)}, s32[2,128,2]{1,2,0:T(2,128)}, u32[]{:S(2)}) copy-start(s32[2,128,2]{1,2,0:T(2,128)} %param.23) | copy-start | bytes 6148
  0.0 11.1 %copy-start.3 = (s32[2]{0:T(128)S(1)}, s32[2]{0:T(128)}, u32[]{:S(2)}) copy-start(s32[2]{0:T(128)} %param.22) | copy-start | bytes 28
  0.0 22.9 %copy-start.1 = (f32[2048]{0:T(1024)S(1)}, f32[2048]{0:T(1024)}, u32[]{:S(2)}) copy-start(f32[2048]{0:T(1024)} %param.33) | copy-start | bytes 24580
  9.6 3.0 %collective-permute-start = (bf16[256,1024]{1,0:T(8,128)(2,1)S(1)}, bf16[256,1024]{1,0:T(8,128)(2,1)S(1)}, u32[]{:S(2)}, u32[]{:S(2)}) collective-permute-start(bf16[256,1024]{1,0:T(8,128)(2,1)S(1)} %get-tuple-element.16), channel_id=1, source_target_pairs={{0,32},{32,0},{64,96},{96,64},{1,33},{33,1},{65,97},{97,65},{2,34}... | collective-permute-start | bytes 1572872 | tf_op jit(solution)/shard_map/head_sum/ppermute | solution.py:580
  11.8 22.9 %collective-permute-start.5 = (bf16[1,2048,512]{2,1,0:T(8,128)(2,1)}, bf16[1,2048,512]{2,1,0:T(8,128)(2,1)}, u32[]{:S(2)}, u32[]{:S(2)}) collective-permute-start(bf16[1,2048,512]{2,1,0:T(8,128)(2,1)} %wg0_h.1), channel_id=1, source_target_pairs={{0,32},{32,0},{64,96},{96,64},{1,33},{33,1},{65,97},{97,65},{2,34}... | collective-permute-start | bytes 6291464 | tf_op jit(solution)/shard_map/sibling_weights/ppermute | solution.py:588
  12.0 22.8 %collective-permute-start.6 = (bf16[1,2048,512]{2,1,0:T(8,128)(2,1)}, bf16[1,2048,512]{2,1,0:T(8,128)(2,1)}, u32[]{:S(2)}, u32[]{:S(2)}) collective-permute-start(bf16[1,2048,512]{2,1,0:T(8,128)(2,1)} %wu0_h.1), channel_id=1, source_target_pairs={{0,32},{32,0},{64,96},{96,64},{1,33},{33,1},{65,97},{97,65},{2,34}... | collective-permute-start | bytes 6291464 | tf_op jit(solution)/shard_map/sibling_weights/ppermute | solution.py:588
  12.4 22.3 %collective-permute-start.7 = (bf16[1,512,2048]{2,1,0:T(8,128)(2,1)}, bf16[1,512,2048]{2,1,0:T(8,128)(2,1)}, u32[]{:S(2)}, u32[]{:S(2)}) collective-permute-start(bf16[1,512,2048]{2,1,0:T(8,128)(2,1)} %wd0_h.1), channel_id=1, source_target_pairs={{0,32},{32,0},{64,96},{96,64},{1,33},{33,1},{65,97},{97,65},{2,34}... | collective-permute-start | bytes 6291464 | tf_op jit(solution)/shard_map/sibling_weights/ppermute | solution.py:588
  12.7 10.1 %collective-permute-start.1 = (bf16[256,512]{1,0:T(8,128)(2,1)S(1)}, bf16[256,512]{1,0:T(8,128)(2,1)S(1)}, u32[]{:S(2)}, u32[]{:S(2)}) collective-permute-start(bf16[256,512]{1,0:T(8,128)(2,1)S(1)} %add_convert_fusion), channel_id=1, source_target_pairs={{0,64},{32,96},{64,0},{96,32},{1,65},{33,97},{65,1},{97,33},{2,66}... | collective-permute-start | bytes 786440 | tf_op jit(solution)/shard_map/head_sum/ppermute | solution.py:582
  24.5 35.2 %all-to-all-start = ((bf16[128,8,768]{2,1,0:T(8,128)(2,1)}), bf16[128,8,768]{2,1,0:T(8,128)(2,1)S(1)}, u32[]{:S(2)}, u32[]{:S(2)}) async-start(bf16[128,8,768]{2,1,0:T(8,128)(2,1)} %bitcast.20), calls=%async_computation | async-start | bytes 3145728 | tf_op jit(solution)/shard_map/dispatch/all_to_all | solution.py:591
  68.2 4.0 %copy-start = (bf16[2048,32]{0,1:T(8,128)(2,1)S(1)}, bf16[2048,32]{0,1:T(8,128)(2,1)}, u32[]{:S(2)}) copy-start(bf16[2048,32]{0,1:T(8,128)(2,1)} %param.34) | copy-start | bytes 393220
  68.2 29.1 %all-to-all-start.1 = ((bf16[128,8,768]{2,1,0:T(8,128)(2,1)}), bf16[128,8,768]{2,1,0:T(8,128)(2,1)S(1)}, u32[]{:S(2)}, u32[]{:S(2)}) async-start(bf16[128,8,768]{2,1,0:T(8,128)(2,1)} %bitcast.19), calls=%async_computation.1 | async-start | bytes 3145728 | tf_op jit(solution)/shard_map/experts/all_to_all | solution.py:599
  72.8 5.6 %collective-permute-start.4 = (f32[8,256]{1,0:T(8,128)S(1)}, f32[8,256]{1,0:T(8,128)S(1)}, u32[]{:S(2)}, u32[]{:S(2)}) collective-permute-start(f32[8,256]{1,0:T(8,128)S(1)} %router.1.p0), channel_id=1, source_target_pairs={{0,96},{32,64},{64,32},{96,0},{1,97},{33,65},{65,33},{97,1},{2,98}... | collective-permute-start | bytes 24584 | tf_op jit(solution)/shard_map/router/ppermute | solution.py:594
  76.5 5.2 %collective-permute-start.3 = (f32[8,256]{1,0:T(8,128)S(1)}, f32[8,256]{1,0:T(8,128)S(1)}, u32[]{:S(2)}, u32[]{:S(2)}) collective-permute-start(f32[8,256]{1,0:T(8,128)S(1)} %router.1.p0), channel_id=1, source_target_pairs={{0,64},{32,96},{64,0},{96,32},{1,65},{33,97},{65,1},{97,33},{2,66}... | collective-permute-start | bytes 24584 | tf_op jit(solution)/shard_map/router/ppermute | solution.py:594
  76.9 4.8 %collective-permute-start.2 = (f32[8,256]{1,0:T(8,128)S(1)}, f32[8,256]{1,0:T(8,128)S(1)}, u32[]{:S(2)}, u32[]{:S(2)}) collective-permute-start(f32[8,256]{1,0:T(8,128)S(1)} %router.1.p0), channel_id=1, source_target_pairs={{0,32},{32,0},{64,96},{96,64},{1,33},{33,1},{65,97},{97,65},{2,34}... | collective-permute-start | bytes 24584 | tf_op jit(solution)/shard_map/router/ppermute | solution.py:594
